TPU v7x, 512 devices: a whole 4x8x8 slice. The times are simulated.
512 devices in a mesh: dp: 32 (over x, y), tensor: 16 (over z, core).
Axes of the slice: x: 4, y: 8, z: 8, core: 2. Of those that a mesh axis runs over, the one named last changes fastest.
Arguments:
- grad: bfloat16 [4096, 28672], P('tensor', 'dp'), may hold values from -6 to 6
- error: float32 [4096, 28672], P('tensor', 'dp'), may hold values from -4 to 4
- q_start: bfloat16 [14336, 64], replicated, may hold values from -0.046875 to 0.046875
Outputs:
- new_error: float32 [4096, 28672], P('tensor', 'dp')
- q_new: float32 [14336, 64], P(('dp', 'tensor'))
All inputs are finite; a program needn't handle non-finite values.
Results may differ from a plain program's by a relative error of at most 0.00045.
Values sent between devices are 32-bit elements; how exact they have to be, the bound alone decides.
No kernel may reach another device: no remote copies, remote signals or barrier semaphores. Data moves between devices by JAX's collectives and lax.ppermute only.
A program may use at most 64 MiB of HBM per device.

v0:
```python
import jax
import jax.numpy as jnp
from jax import lax
from jax.sharding import PartitionSpec as P

REPLICAS = 2


def shards(grad, error, q_start):
    highest = lax.Precision.HIGHEST
    n_members = lax.axis_size("dp")
    merged = grad.astype(jnp.float32) + error
    own_cols = merged.shape[1]
    total_cols = q_start.shape[0]
    col_start = lax.axis_index("dp") % (n_members // REPLICAS) * own_cols
    q_local = lax.dynamic_slice_in_dim(q_start, col_start, own_cols, 0).astype(jnp.float32)
    p_own = jnp.dot(merged, q_local, precision=highest)
    p_mean = lax.psum(p_own, "dp") / REPLICAS
    gram = lax.psum(jnp.dot(p_mean.T, p_mean, precision=highest), "tensor")
    lower = jnp.linalg.cholesky(gram)
    basis = lax.linalg.triangular_solve(
        lower, p_mean, left_side=False, lower=True, transpose_a=True
    )
    local_term = jnp.dot(merged.T, basis, precision=highest)
    padded = jnp.zeros((total_cols, basis.shape[1]), jnp.float32)
    padded = lax.dynamic_update_slice(padded, local_term, (col_start, jnp.zeros((), jnp.int32)))
    q_sum = lax.psum_scatter(padded, ("dp", "tensor"), scatter_dimension=0, tiled=True)
    q_new = q_sum / REPLICAS
    whole_q = lax.all_gather(q_new, ("dp", "tensor"), axis=0, tiled=True)
    own_q = lax.dynamic_slice_in_dim(whole_q, col_start, own_cols, 0)
    new_error = merged - jnp.dot(basis, own_q.T, precision=highest)
    return (new_error, q_new)


def solution(mesh):
    return jax.shard_map(
        shards,
        mesh=mesh,
        in_specs=(P("tensor", "dp"), P("tensor", "dp"), P()),
        out_specs=(P("tensor", "dp"), P(("dp", "tensor"), None)),
        check_vma=False,
    )
```

profile of v0, /device:TPU:1, one launch (start us, length us, event | category | flops | bytes accessed | tf_op | source)
XLA Modules:
  0.0 2387.9 jit_solution(726706539211577491)
XLA Ops:
  7.3 1.4 copy-done
  8.7 2.5 fusion.2
  11.3 152.6 %all-reduce.4.cloned.1.call-done = f32[256,64]{0,1:T(8,128)} async-done(((f32[256,64]{0,1:T(8,128)}), f32[256,64]{0,1:T(8,128)}) %all-reduce.4.cloned.1.call-update) | async-done | bytes 65552 | tf_op jit(solution)/shard_map/psum | solution.py:18
  165.0 47.9 %psum.15 = f32[64,64]{0,1:T(8,128)S(1)} all-reduce(f32[64,64]{0,1:T(8,128)S(1)} %fusion.6), channel_id=1, replica_groups=mesh['dp'=32,'tensor'=16] {'tensor'}, use_global_device_ids=true, to_apply=%region_1.2 | all-reduce | flops 4096 | bytes 32768 | tf_op jit(solution)/shard_map/psum | solution.py:19
  213.0 5.8 cholesky.16
  220.2 4.9 custom-call.6
  226.2 3.2 broadcast_in_dim.5
  229.4 2.4 convolution_dynamic-update-slice_fusion
  231.8 1318.2 %fusion = f32[32,64]{1,0:T(8,128)S(1)} fusion(f32[14336,64]{1,0:T(8,128)} %convolution_dynamic-update-slice_fusion), kind=kCustom, calls=%all-reduce-scatter | all-reduce-scatter fusion | flops 1048577 | bytes 3678208
  1565.7 49.3 %collective-permute-start.51 = (f32[32,64]{1,0:T(8,128)S(1)}, f32[32,64]{1,0:T(8,128)S(1)}, u32[]{:S(2)}, u32[]{:S(2)}) collective-permute-start(f32[32,64]{1,0:T(8,128)S(1)} %fusion), channel_id=1, source_target_pairs={{0,52},{1,53},{2,54},{3,55},{4,56},{5,57},{6,58},{7,59},{8,60},{9,... | collective-permute-start | bytes 24584
  1615.0 1.9 collective-permute-start.50
  1618.2 1.7 collective-permute-start.48
  1619.9 2.2 collective-permute-start.47
  1623.4 1.8 collective-permute-start.45
  1625.2 1.9 collective-permute-start.44
  1627.1 5.3 collective-permute-start.43
  1632.5 3.6 collective-permute-start.42
  1636.1 4.1 collective-permute-start.41
  1640.3 3.2 collective-permute-start.40
  1643.5 3.5 collective-permute-start.39
  1647.0 4.3 collective-permute-start.38
  1651.3 2.2 collective-permute-start.37
  1653.6 2.6 collective-permute-start.36
  1656.2 3.2 collective-permute-start.35
  1659.4 1.9 collective-permute-start.34
  1661.3 2.7 collective-permute-start.33
  1664.0 1.6 collective-permute-start.32
  1665.6 2.6 collective-permute-start.31
  1668.2 1.6 collective-permute-start.30
  1669.9 3.1 collective-permute-start.29
  1673.0 4.4 collective-permute-start.28
  1677.4 16.7 collective-permute-start.27
  1694.2 16.7 collective-permute-start.26
  1711.0 16.7 collective-permute-start.25
  1727.7 16.7 collective-permute-start.24
  1744.5 16.7 collective-permute-start.23
  1761.2 16.7 collective-permute-start.22
  1778.0 16.7 collective-permute-start.21
  1794.8 16.7 collective-permute-start.20
  1811.5 16.7 collective-permute-start.19
  1828.3 16.7 collective-permute-start.18
  1845.1 16.7 collective-permute-start.17
  1861.8 16.7 collective-permute-start.16
  1878.6 16.7 collective-permute-start.15
  1895.4 16.7 collective-permute-start.14
  1912.1 16.7 collective-permute-start.13
  1928.9 16.7 collective-permute-start.12
  1945.7 16.7 collective-permute-start.11
  1962.4 16.7 collective-permute-start.10
  1979.2 16.7 collective-permute-start.9
  1996.0 17.3 collective-permute-start.8
  2013.3 16.8 collective-permute-start.7
  2030.1 16.8 collective-permute-start.6
  2046.8 16.8 collective-permute-start.5
  2063.6 16.8 collective-permute-start.4
  2080.4 16.8 collective-permute-start.3
  2097.1 16.7 collective-permute-start.2
  2113.9 16.8 collective-permute-start.1
  2130.7 16.3 collective-permute-start
  2147.4 4.3 collective-permute-done
  2151.8 88.3 %concatenate = f32[2076,64]{1,0:T(8,128)} concatenate(f32[28,64]{1,0:T(8,128)S(1)} %collective-permute-done.63, f32[32,64]{1,0:T(8,128)S(1)} %collective-permute-done.62, f32[32,64]{1,0:T(8,128)S(1)} %collective-permute-done.61, f32[32,64]{1,0:T(8,128)S(1)} %collective-permute-done.60, f32[32,64]{1,0:T(8,128)S(1)} %collective-permute-done.59, ...), dimensions={0} | concatenate | bytes 1062912
  2242.8 126.5 %all-gather.3.cloned.1.call-done = f32[512,28,64]{2,1,0:T(8,128)} async-done(((f32[1,28,64]{2,1,0:T(8,128)}), f32[512,28,64]{2,1,0:T(8,128)}) %all-gather.3.cloned.1.call-update) | async-done | bytes 3670032 | tf_op jit(solution)/shard_map/all_gather | solution.py:29
  2369.3 8.8 reshape.14
  2378.1 3.0 convolution_subtract_fusion
  (174 shorter events, 24.8 us)
Async XLA Ops:
  7.2 156.7 %all-reduce.4.cloned.1.call-start = ((), (), s32[]{:S(2)}) async-start(), calls=%async_computation | async-start | bytes 131072 | tf_op jit(solution)/shard_map/psum | solution.py:18
  11.2 2358.0 %all-gather.3.cloned.1.call-start = ((), (), s32[]{:S(2)}) async-start(), calls=%async_computation.1 | async-start | bytes 8404992 | tf_op jit(solution)/shard_map/all_gather | solution.py:29
  1550.0 7.8 collective-permute-start.62
  1551.3 7.8 collective-permute-start.61
  1552.6 7.8 collective-permute-start.60
  1555.2 6.5 collective-permute-start.59
  1556.5 6.5 collective-permute-start.58
  1557.9 6.5 collective-permute-start.57
  1560.5 54.5 %collective-permute-start.55 = (f32[32,64]{1,0:T(8,128)S(1)}, f32[32,64]{1,0:T(8,128)S(1)}, u32[]{:S(2)}, u32[]{:S(2)}) collective-permute-start(f32[32,64]{1,0:T(8,128)S(1)} %fusion), channel_id=1, source_target_pairs={{0,56},{1,57},{2,58},{3,59},{4,60},{5,61},{6,62},{7,63},{8,64},{9,... | collective-permute-start | bytes 24584
  1561.8 55.1 %collective-permute-start.54 = (f32[32,64]{1,0:T(8,128)S(1)}, f32[32,64]{1,0:T(8,128)S(1)}, u32[]{:S(2)}, u32[]{:S(2)}) collective-permute-start(f32[32,64]{1,0:T(8,128)S(1)} %fusion), channel_id=1, source_target_pairs={{0,55},{1,56},{2,57},{3,58},{4,59},{5,60},{6,61},{7,62},{8,63},{9,... | collective-permute-start | bytes 24584
  1563.1 55.1 %collective-permute-start.53 = (f32[32,64]{1,0:T(8,128)S(1)}, f32[32,64]{1,0:T(8,128)S(1)}, u32[]{:S(2)}, u32[]{:S(2)}) collective-permute-start(f32[32,64]{1,0:T(8,128)S(1)} %fusion), channel_id=1, source_target_pairs={{0,54},{1,55},{2,56},{3,57},{4,58},{5,59},{6,60},{7,61},{8,62},{9,... | collective-permute-start | bytes 24584
  1564.4 55.5 %collective-permute-start.52 = (f32[32,64]{1,0:T(8,128)S(1)}, f32[32,64]{1,0:T(8,128)S(1)}, u32[]{:S(2)}, u32[]{:S(2)}) collective-permute-start(f32[32,64]{1,0:T(8,128)S(1)} %fusion), channel_id=1, source_target_pairs={{0,53},{1,54},{2,55},{3,56},{4,57},{5,58},{6,59},{7,60},{8,61},{9,... | collective-permute-start | bytes 24584
  1565.7 56.4 %collective-permute-start.51 = (f32[32,64]{1,0:T(8,128)S(1)}, f32[32,64]{1,0:T(8,128)S(1)}, u32[]{:S(2)}, u32[]{:S(2)}) collective-permute-start(f32[32,64]{1,0:T(8,128)S(1)} %fusion), channel_id=1, source_target_pairs={{0,52},{1,53},{2,54},{3,55},{4,56},{5,57},{6,58},{7,59},{8,60},{9,... | collective-permute-start | bytes 24584
  1615.0 8.4 collective-permute-start.50
  1616.9 8.3 collective-permute-start.49
  1618.2 8.9 collective-permute-start.48
  1619.9 12.6 collective-permute-start.47
  1622.1 14.0 collective-permute-start.46
  1623.4 16.8 collective-permute-start.45
  1625.2 18.3 collective-permute-start.44
  1627.1 19.9 collective-permute-start.43
  1632.5 18.8 collective-permute-start.42
  1636.1 17.5 collective-permute-start.41
  1640.3 15.9 collective-permute-start.40
  1643.5 15.9 collective-permute-start.39
  1647.0 14.3 collective-permute-start.38
  1651.3 12.7 collective-permute-start.37
  1653.6 12.0 collective-permute-start.36
  1656.2 12.0 collective-permute-start.35
  1659.4 10.5 collective-permute-start.34
  1661.3 11.7 collective-permute-start.33
  1664.0 13.4 collective-permute-start.32
  1665.6 28.5 %collective-permute-start.31 = (f32[32,64]{1,0:T(8,128)S(1)}, f32[32,64]{1,0:T(8,128)S(1)}, u32[]{:S(2)}, u32[]{:S(2)}) collective-permute-start(f32[32,64]{1,0:T(8,128)S(1)} %fusion), channel_id=1, source_target_pairs={{0,32},{1,33},{2,34},{3,35},{4,36},{5,37},{6,38},{7,39},{8,40},{9,... | collective-permute-start | bytes 24584
  1668.2 42.7 %collective-permute-start.30 = (f32[32,64]{1,0:T(8,128)S(1)}, f32[32,64]{1,0:T(8,128)S(1)}, u32[]{:S(2)}, u32[]{:S(2)}) collective-permute-start(f32[32,64]{1,0:T(8,128)S(1)} %fusion), channel_id=1, source_target_pairs={{0,31},{1,32},{2,33},{3,34},{4,35},{5,36},{6,37},{7,38},{8,39},{9,... | collective-permute-start | bytes 24584
  1669.9 57.8 %collective-permute-start.29 = (f32[32,64]{1,0:T(8,128)S(1)}, f32[32,64]{1,0:T(8,128)S(1)}, u32[]{:S(2)}, u32[]{:S(2)}) collective-permute-start(f32[32,64]{1,0:T(8,128)S(1)} %fusion), channel_id=1, source_target_pairs={{0,30},{1,31},{2,32},{3,33},{4,34},{5,35},{6,36},{7,37},{8,38},{9,... | collective-permute-start | bytes 24584
  1673.0 71.4 %collective-permute-start.28 = (f32[32,64]{1,0:T(8,128)S(1)}, f32[32,64]{1,0:T(8,128)S(1)}, u32[]{:S(2)}, u32[]{:S(2)}) collective-permute-start(f32[32,64]{1,0:T(8,128)S(1)} %fusion), channel_id=1, source_target_pairs={{0,29},{1,30},{2,31},{3,32},{4,33},{5,34},{6,35},{7,36},{8,37},{9,... | collective-permute-start | bytes 24584
  1677.4 83.8 %collective-permute-start.27 = (f32[32,64]{1,0:T(8,128)S(1)}, f32[32,64]{1,0:T(8,128)S(1)}, u32[]{:S(2)}, u32[]{:S(2)}) collective-permute-start(f32[32,64]{1,0:T(8,128)S(1)} %fusion), channel_id=1, source_target_pairs={{0,28},{1,29},{2,30},{3,31},{4,32},{5,33},{6,34},{7,35},{8,36},{9,... | collective-permute-start | bytes 24584
  1694.2 83.8 %collective-permute-start.26 = (f32[32,64]{1,0:T(8,128)S(1)}, f32[32,64]{1,0:T(8,128)S(1)}, u32[]{:S(2)}, u32[]{:S(2)}) collective-permute-start(f32[32,64]{1,0:T(8,128)S(1)} %fusion), channel_id=1, source_target_pairs={{0,27},{1,28},{2,29},{3,30},{4,31},{5,32},{6,33},{7,34},{8,35},{9,... | collective-permute-start | bytes 24584
  1711.0 83.8 %collective-permute-start.25 = (f32[32,64]{1,0:T(8,128)S(1)}, f32[32,64]{1,0:T(8,128)S(1)}, u32[]{:S(2)}, u32[]{:S(2)}) collective-permute-start(f32[32,64]{1,0:T(8,128)S(1)} %fusion), channel_id=1, source_target_pairs={{0,26},{1,27},{2,28},{3,29},{4,30},{5,31},{6,32},{7,33},{8,34},{9,... | collective-permute-start | bytes 24584
  1727.7 83.8 %collective-permute-start.24 = (f32[32,64]{1,0:T(8,128)S(1)}, f32[32,64]{1,0:T(8,128)S(1)}, u32[]{:S(2)}, u32[]{:S(2)}) collective-permute-start(f32[32,64]{1,0:T(8,128)S(1)} %fusion), channel_id=1, source_target_pairs={{0,25},{1,26},{2,27},{3,28},{4,29},{5,30},{6,31},{7,32},{8,33},{9,... | collective-permute-start | bytes 24584
  1744.5 83.8 %collective-permute-start.23 = (f32[32,64]{1,0:T(8,128)S(1)}, f32[32,64]{1,0:T(8,128)S(1)}, u32[]{:S(2)}, u32[]{:S(2)}) collective-permute-start(f32[32,64]{1,0:T(8,128)S(1)} %fusion), channel_id=1, source_target_pairs={{0,24},{1,25},{2,26},{3,27},{4,28},{5,29},{6,30},{7,31},{8,32},{9,... | collective-permute-start | bytes 24584
  1761.2 83.8 %collective-permute-start.22 = (f32[32,64]{1,0:T(8,128)S(1)}, f32[32,64]{1,0:T(8,128)S(1)}, u32[]{:S(2)}, u32[]{:S(2)}) collective-permute-start(f32[32,64]{1,0:T(8,128)S(1)} %fusion), channel_id=1, source_target_pairs={{0,23},{1,24},{2,25},{3,26},{4,27},{5,28},{6,29},{7,30},{8,31},{9,... | collective-permute-start | bytes 24584
  1778.0 83.8 %collective-permute-start.21 = (f32[32,64]{1,0:T(8,128)S(1)}, f32[32,64]{1,0:T(8,128)S(1)}, u32[]{:S(2)}, u32[]{:S(2)}) collective-permute-start(f32[32,64]{1,0:T(8,128)S(1)} %fusion), channel_id=1, source_target_pairs={{0,22},{1,23},{2,24},{3,25},{4,26},{5,27},{6,28},{7,29},{8,30},{9,... | collective-permute-start | bytes 24584
  1794.8 83.8 %collective-permute-start.20 = (f32[32,64]{1,0:T(8,128)S(1)}, f32[32,64]{1,0:T(8,128)S(1)}, u32[]{:S(2)}, u32[]{:S(2)}) collective-permute-start(f32[32,64]{1,0:T(8,128)S(1)} %fusion), channel_id=1, source_target_pairs={{0,21},{1,22},{2,23},{3,24},{4,25},{5,26},{6,27},{7,28},{8,29},{9,... | collective-permute-start | bytes 24584
  1811.5 83.8 %collective-permute-start.19 = (f32[32,64]{1,0:T(8,128)S(1)}, f32[32,64]{1,0:T(8,128)S(1)}, u32[]{:S(2)}, u32[]{:S(2)}) collective-permute-start(f32[32,64]{1,0:T(8,128)S(1)} %fusion), channel_id=1, source_target_pairs={{0,20},{1,21},{2,22},{3,23},{4,24},{5,25},{6,26},{7,27},{8,28},{9,... | collective-permute-start | bytes 24584
  1828.3 83.8 %collective-permute-start.18 = (f32[32,64]{1,0:T(8,128)S(1)}, f32[32,64]{1,0:T(8,128)S(1)}, u32[]{:S(2)}, u32[]{:S(2)}) collective-permute-start(f32[32,64]{1,0:T(8,128)S(1)} %fusion), channel_id=1, source_target_pairs={{0,19},{1,20},{2,21},{3,22},{4,23},{5,24},{6,25},{7,26},{8,27},{9,... | collective-permute-start | bytes 24584
  1845.1 83.8 %collective-permute-start.17 = (f32[32,64]{1,0:T(8,128)S(1)}, f32[32,64]{1,0:T(8,128)S(1)}, u32[]{:S(2)}, u32[]{:S(2)}) collective-permute-start(f32[32,64]{1,0:T(8,128)S(1)} %fusion), channel_id=1, source_target_pairs={{0,18},{1,19},{2,20},{3,21},{4,22},{5,23},{6,24},{7,25},{8,26},{9,... | collective-permute-start | bytes 24584
  1861.8 83.8 %collective-permute-start.16 = (f32[32,64]{1,0:T(8,128)S(1)}, f32[32,64]{1,0:T(8,128)S(1)}, u32[]{:S(2)}, u32[]{:S(2)}) collective-permute-start(f32[32,64]{1,0:T(8,128)S(1)} %fusion), channel_id=1, source_target_pairs={{0,17},{1,18},{2,19},{3,20},{4,21},{5,22},{6,23},{7,24},{8,25},{9,... | collective-permute-start | bytes 24584
  1878.6 83.8 %collective-permute-start.15 = (f32[32,64]{1,0:T(8,128)S(1)}, f32[32,64]{1,0:T(8,128)S(1)}, u32[]{:S(2)}, u32[]{:S(2)}) collective-permute-start(f32[32,64]{1,0:T(8,128)S(1)} %fusion), channel_id=1, source_target_pairs={{0,16},{1,17},{2,18},{3,19},{4,20},{5,21},{6,22},{7,23},{8,24},{9,... | collective-permute-start | bytes 24584
  1895.4 83.8 %collective-permute-start.14 = (f32[32,64]{1,0:T(8,128)S(1)}, f32[32,64]{1,0:T(8,128)S(1)}, u32[]{:S(2)}, u32[]{:S(2)}) collective-permute-start(f32[32,64]{1,0:T(8,128)S(1)} %fusion), channel_id=1, source_target_pairs={{0,15},{1,16},{2,17},{3,18},{4,19},{5,20},{6,21},{7,22},{8,23},{9,... | collective-permute-start | bytes 24584
  1912.1 83.8 %collective-permute-start.13 = (f32[32,64]{1,0:T(8,128)S(1)}, f32[32,64]{1,0:T(8,128)S(1)}, u32[]{:S(2)}, u32[]{:S(2)}) collective-permute-start(f32[32,64]{1,0:T(8,128)S(1)} %fusion), channel_id=1, source_target_pairs={{0,14},{1,15},{2,16},{3,17},{4,18},{5,19},{6,20},{7,21},{8,22},{9,... | collective-permute-start | bytes 24584
  1928.9 84.4 %collective-permute-start.12 = (f32[32,64]{1,0:T(8,128)S(1)}, f32[32,64]{1,0:T(8,128)S(1)}, u32[]{:S(2)}, u32[]{:S(2)}) collective-permute-start(f32[32,64]{1,0:T(8,128)S(1)} %fusion), channel_id=1, source_target_pairs={{0,13},{1,14},{2,15},{3,16},{4,17},{5,18},{6,19},{7,20},{8,21},{9,... | collective-permute-start | bytes 24584
  1945.7 84.4 %collective-permute-start.11 = (f32[32,64]{1,0:T(8,128)S(1)}, f32[32,64]{1,0:T(8,128)S(1)}, u32[]{:S(2)}, u32[]{:S(2)}) collective-permute-start(f32[32,64]{1,0:T(8,128)S(1)} %fusion), channel_id=1, source_target_pairs={{0,12},{1,13},{2,14},{3,15},{4,16},{5,17},{6,18},{7,19},{8,20},{9,... | collective-permute-start | bytes 24584
  1962.4 84.4 %collective-permute-start.10 = (f32[32,64]{1,0:T(8,128)S(1)}, f32[32,64]{1,0:T(8,128)S(1)}, u32[]{:S(2)}, u32[]{:S(2)}) collective-permute-start(f32[32,64]{1,0:T(8,128)S(1)} %fusion), channel_id=1, source_target_pairs={{0,11},{1,12},{2,13},{3,14},{4,15},{5,16},{6,17},{7,18},{8,19},{9,... | collective-permute-start | bytes 24584
  1979.2 84.4 %collective-permute-start.9 = (f32[32,64]{1,0:T(8,128)S(1)}, f32[32,64]{1,0:T(8,128)S(1)}, u32[]{:S(2)}, u32[]{:S(2)}) collective-permute-start(f32[32,64]{1,0:T(8,128)S(1)} %fusion), channel_id=1, source_target_pairs={{0,10},{1,11},{2,12},{3,13},{4,14},{5,15},{6,16},{7,17},{8,18},{9,... | collective-permute-start | bytes 24584
  1996.0 84.4 %collective-permute-start.8 = (f32[32,64]{1,0:T(8,128)S(1)}, f32[32,64]{1,0:T(8,128)}, u32[]{:S(2)}, u32[]{:S(2)}) collective-permute-start(f32[32,64]{1,0:T(8,128)S(1)} %fusion), channel_id=1, source_target_pairs={{0,9},{1,10},{2,11},{3,12},{4,13},{5,14},{6,15},{7,16},{8,17},{9,1... | collective-permute-start | bytes 24584
  2013.3 83.8 %collective-permute-start.7 = (f32[32,64]{1,0:T(8,128)S(1)}, f32[32,64]{1,0:T(8,128)}, u32[]{:S(2)}, u32[]{:S(2)}) collective-permute-start(f32[32,64]{1,0:T(8,128)S(1)} %fusion), channel_id=1, source_target_pairs={{0,8},{1,9},{2,10},{3,11},{4,12},{5,13},{6,14},{7,15},{8,16},{9,17... | collective-permute-start | bytes 24584
  2030.1 83.8 %collective-permute-start.6 = (f32[32,64]{1,0:T(8,128)S(1)}, f32[32,64]{1,0:T(8,128)}, u32[]{:S(2)}, u32[]{:S(2)}) collective-permute-start(f32[32,64]{1,0:T(8,128)S(1)} %fusion), channel_id=1, source_target_pairs={{0,7},{1,8},{2,9},{3,10},{4,11},{5,12},{6,13},{7,14},{8,15},{9,16}... | collective-permute-start | bytes 24584
  2046.8 83.8 %collective-permute-start.5 = (f32[32,64]{1,0:T(8,128)S(1)}, f32[32,64]{1,0:T(8,128)}, u32[]{:S(2)}, u32[]{:S(2)}) collective-permute-start(f32[32,64]{1,0:T(8,128)S(1)} %fusion), channel_id=1, source_target_pairs={{0,6},{1,7},{2,8},{3,9},{4,10},{5,11},{6,12},{7,13},{8,14},{9,15},... | collective-permute-start | bytes 24584
  2063.6 83.8 %collective-permute-start.4 = (f32[32,64]{1,0:T(8,128)S(1)}, f32[32,64]{1,0:T(8,128)}, u32[]{:S(2)}, u32[]{:S(2)}) collective-permute-start(f32[32,64]{1,0:T(8,128)S(1)} %fusion), channel_id=1, source_target_pairs={{0,5},{1,6},{2,7},{3,8},{4,9},{5,10},{6,11},{7,12},{8,13},{9,14},{... | collective-permute-start | bytes 24584
  2080.4 67.0 %collective-permute-start.3 = (f32[32,64]{1,0:T(8,128)S(1)}, f32[32,64]{1,0:T(8,128)}, u32[]{:S(2)}, u32[]{:S(2)}) collective-permute-start(f32[32,64]{1,0:T(8,128)S(1)} %fusion), channel_id=1, source_target_pairs={{0,4},{1,5},{2,6},{3,7},{4,8},{5,9},{6,10},{7,11},{8,12},{9,13},{1... | collective-permute-start | bytes 24584
  2097.1 50.3 %collective-permute-start.2 = (f32[32,64]{1,0:T(8,128)S(1)}, f32[32,64]{1,0:T(8,128)}, u32[]{:S(2)}, u32[]{:S(2)}) collective-permute-start(f32[32,64]{1,0:T(8,128)S(1)} %fusion), channel_id=1, source_target_pairs={{0,3},{1,4},{2,5},{3,6},{4,7},{5,8},{6,9},{7,10},{8,11},{9,12},{10... | collective-permute-start | bytes 24584
  2113.9 33.5 %collective-permute-start.1 = (f32[32,64]{1,0:T(8,128)S(1)}, f32[32,64]{1,0:T(8,128)}, u32[]{:S(2)}, u32[]{:S(2)}) collective-permute-start(f32[32,64]{1,0:T(8,128)S(1)} %fusion), channel_id=1, source_target_pairs={{0,2},{1,3},{2,4},{3,5},{4,6},{5,7},{6,8},{7,9},{8,10},{9,11},{10,... | collective-permute-start | bytes 24584
  2130.7 21.1 collective-permute-start
  (44 other events, 14469.8 us)
Sparse Core Ops, SparseCore 0:
  12.1 151.7 all-reduce.3
  2241.6 127.6 all-gather.2
where the time goes:
time: 2400 us; the launch traced here: 2390 us
  blocking collectives  1370 us (57%)
  starting transfers between devices  596 us (25%)
  waiting for transfers between devices  284 us (12%)
  local copies, waits for them, and re-layouts  102 us (4%)
    unnamed x1, blocking collectives  1320 us
    unnamed x64, starting transfers between devices  596 us
    psum x1, waiting for transfers between devices, shards(): p_mean = lax.psum(p_own, 'dp') / REPLICAS  153 us
    all_gather x1, waiting for transfers between devices, shards(): whole_q = lax.all_gather(q_new, ('dp', 'tensor'), axis=0, tiled=True)  126 us
    unnamed x87, local copies, waits for them, and re-layouts  98.7 us
  transfers between devices with their start and end apart: 66, of which 3 were waited for; matrix products, arithmetic and copies ran while one was open for 0% of the time, Pallas kernels for 0%

commit v1 on v0

v1 whole, which is shorter than its diff:
```python
import jax
import jax.numpy as jnp
from jax import lax
from jax.experimental import pallas as pl
from jax.experimental.pallas import tpu as pltpu
from jax.sharding import Mesh, PartitionSpec as P

REPLICAS = 2
RANK = 64
PARTS = 32
OWN = 28
SLOT = 16
NT = (((1,), (1,)), ((), ()))
NN = (((1,), (0,)), ((), ()))
BF16 = jnp.bfloat16
F32 = jnp.float32


def split(value):
    high = value.astype(BF16)
    return high, (value - high.astype(F32)).astype(BF16)


def dot(a, b, dims):
    return lax.dot_general(a, b, dims, preferred_element_type=F32)


def dot3(a, b, dims):
    a_high, a_low = split(a)
    b_high, b_low = split(b)
    return dot(a_high, b_high, dims) + (dot(a_high, b_low, dims) + dot(a_low, b_high, dims))


def left_kernel(col_ref, grad_ref, error_ref, q_ref, out_ref):
    high, low = split(grad_ref[...].astype(F32) + error_ref[...])
    q = q_ref[...]
    p = dot(high, q, NN) + dot(low, q, NN)
    half = p.shape[0] // 2
    out_ref[...] = jnp.concatenate([p[:half], p[half:]], axis=1)


def arrange_kernel(grad_ref, error_ref, first_high_ref, first_low_ref, last_high_ref, last_low_ref):
    high, low = split(grad_ref[...].astype(F32) + error_ref[...])
    shape = (PARTS * SLOT, high.shape[1])
    row = lax.broadcasted_iota(jnp.int32, shape, 0)
    col = lax.broadcasted_iota(jnp.int32, shape, 1)
    within = row % SLOT
    place = OWN * (row // SLOT) + within
    first = (col == place).astype(F32).astype(BF16)
    last = ((col == place + SLOT) & (within < OWN - SLOT)).astype(F32).astype(BF16)
    first_high_ref[...] = dot(first, high, NT).astype(BF16)
    first_low_ref[...] = dot(first, low, NT).astype(BF16)
    last_high_ref[...] = dot(last, high, NT).astype(BF16)
    last_low_ref[...] = dot(last, low, NT).astype(BF16)


def sum_left_kernel(in_ref, out_ref):
    rows = in_ref.shape[0]
    total = jnp.sum(in_ref[...].reshape(rows // 8, 8, 128), axis=0)
    total = total + pltpu.roll(total, 4, 0)
    out_ref[...] = jnp.broadcast_to(total[None], (rows // 8, 8, 128)).reshape(rows, 128)


def right_kernel(p_ref, first_high_ref, first_low_ref, last_high_ref, last_low_ref, out_ref, gram_ref):
    top = p_ref[...]
    bottom = pltpu.roll(top, RANK, 1)
    lane = lax.broadcasted_iota(jnp.int32, top.shape, 1)
    lower = lane < RANK
    zero = jnp.zeros_like(top)
    left = jnp.concatenate([jnp.where(lower, top, zero), jnp.where(lower, bottom, zero)], axis=0)
    right = jnp.concatenate([jnp.where(lower, zero, bottom), jnp.where(lower, zero, top)], axis=0)
    left_high, left_low = split(left)
    right_high, right_low = split(right)
    left_both = jnp.concatenate([left_high, left_low], axis=1)
    right_both = jnp.concatenate([right_high, right_low], axis=1)
    both = (
        dot(first_high_ref[...], left_both, NN)
        + dot(last_high_ref[...], right_both, NN)
        + dot(first_low_ref[...], left_both, NN)
        + dot(last_low_ref[...], right_both, NN)
    )
    out_ref[...] = both[:, :128] + both[:, 128:]
    turned = top.T
    turned = jnp.concatenate([turned[:RANK], turned[RANK:]], axis=1)
    gram_ref[...] = dot3(turned, right, NN)
    for k in range(PARTS):
        out_ref[SLOT * k + 12 : SLOT * k + 14, RANK:] = gram_ref[2 * k : 2 * k + 2, RANK:]


def sum_right_kernel(in_ref, out_ref, own_ref):
    total = jnp.sum(in_ref[...].reshape(PARTS, SLOT, 128), axis=0)
    own_ref[...] = total
    out_ref[...] = jnp.broadcast_to(total[None], (PARTS, SLOT, 128)).reshape(PARTS * SLOT, 128)


def eliminate(tiles):
    sub = lax.broadcasted_iota(jnp.int32, (8, 128), 0)
    spread = lambda value: jnp.broadcast_to(value, (8, 128))
    scales = [jnp.zeros((8, 128), F32) for _ in tiles]
    count = len(tiles)
    width = 4
    for start in range(0, RANK, width):
        t = start // 8
        offset = start % 8
        cols = [
            {i: spread(tiles[i][:, RANK + start + q : RANK + start + q + 1]) for i in range(t, count)}
            for q in range(width)
        ]
        rows = [spread(tiles[t][offset + q : offset + q + 1, :]) for q in range(width)]
        for q in range(width):
            row = offset + q
            pivot = spread(cols[q][t][row : row + 1, :])
            inverse = 1.0 / pivot
            root = lax.rsqrt(pivot)
            root = root * (1.5 - 0.5 * pivot * root * root)
            scales[t] = jnp.where(sub == row, root, scales[t])
            scaled = rows[q] * inverse
            factor = dict(cols[q])
            factor[t] = jnp.where(sub > row, cols[q][t], 0.0)
            for q2 in range(q + 1, width):
                entry = spread(cols[q2][t][row : row + 1, :]) * inverse
                rows[q2] = rows[q2] - spread(factor[t][offset + q2 : offset + q2 + 1, :]) * scaled
                for i in range(t, count):
                    cols[q2][i] = cols[q2][i] - factor[i] * entry
            for i in range(t, count):
                tiles[i] = tiles[i] - factor[i] * scaled
    return [tile * scale for tile, scale in zip(tiles, scales)]


def error_kernel(grad_ref, error_ref, p_ref, s_ref, own_ref, error_out_ref, q_out_ref, table_ref, right_ref):
    row = lax.broadcasted_iota(jnp.int32, (RANK, 128), 0)
    lane = lax.broadcasted_iota(jnp.int32, (RANK, 128), 1)
    table_ref[...] = (row == lane).astype(F32)
    for k in range(PARTS):
        table_ref[2 * k : 2 * k + 2, RANK:] = 0.5 * s_ref[SLOT * k + 12 : SLOT * k + 14, RANK:]
    tiles = eliminate([table_ref[8 * i : 8 * i + 8, :] for i in range(RANK // 8)])
    inverse = jnp.where(lane < RANK, jnp.concatenate(tiles, axis=0), 0.0)
    both = jnp.concatenate([inverse, pltpu.roll(inverse, RANK, 1)], axis=0)
    basis = dot3(p_ref[...], both, NT)
    basis = jnp.concatenate([basis[:, :RANK], basis[:, RANK:]], axis=0)
    right = 0.5 * dot3(s_ref[...], both, NT)
    shifted = pltpu.roll(right, RANK, 1)
    for k in range(PARTS):
        right_ref[OWN * k : OWN * k + SLOT, :] = right[SLOT * k : SLOT * k + SLOT, :RANK]
        right_ref[OWN * k + SLOT : OWN * k + OWN, :] = shifted[SLOT * k : SLOT * k + OWN - SLOT, :RANK]
    own = 0.5 * dot3(own_ref[...], both, NT)
    q_out_ref[:SLOT, :] = own[:, :RANK]
    q_out_ref[SLOT:, :] = pltpu.roll(own, RANK, 1)[: OWN - SLOT, :RANK]
    merged = grad_ref[...].astype(F32) + error_ref[...]
    error_out_ref[...] = merged - dot3(basis, right_ref[...], NT)


def shape(*dims, kind=F32):
    return jax.ShapeDtypeStruct(dims, kind)


def params():
    return pltpu.CompilerParams(vmem_limit_bytes=24 * 1024 * 1024)


def shards(grad, error, q_start):
    rows, cols = grad.shape
    col = lax.axis_index("col").astype(jnp.int32).reshape(1)
    with jax.named_scope("left"):
        p_own = pl.pallas_call(
            left_kernel,
            grid_spec=pltpu.PrefetchScalarGridSpec(
                num_scalar_prefetch=1,
                grid=(1,),
                in_specs=[
                    pl.BlockSpec((rows, cols), lambda i, c: (0, 0)),
                    pl.BlockSpec((rows, cols), lambda i, c: (0, 0)),
                    pl.BlockSpec((cols, RANK), lambda i, c: (c[0], 0)),
                ],
                out_specs=pl.BlockSpec((rows // 2, 128), lambda i, c: (0, 0)),
            ),
            out_shape=shape(rows // 2, 128),
            compiler_params=params(),
        )(col, grad, error, q_start)
    with jax.named_scope("left_scatter"):
        p_parts = lax.all_to_all(p_own, ("rep", "col"), 0, 0, tiled=True)
    with jax.named_scope("arrange"):
        arranged = pl.pallas_call(
            arrange_kernel,
            out_shape=[shape(PARTS * SLOT, rows, kind=BF16)] * 4,
            compiler_params=params(),
            cost_estimate=pl.CostEstimate(flops=2 * 4 * 512 * 256 * 896, bytes_accessed=2500000, transcendentals=0),
        )(grad, error)
    with jax.named_scope("left_sum"):
        p_sum = pl.pallas_call(sum_left_kernel, out_shape=shape(rows // 2, 128), compiler_params=params())(p_parts)
    with jax.named_scope("left_gather"):
        p = lax.all_to_all(p_sum, ("rep", "col"), 0, 0, tiled=True)
    with jax.named_scope("right"):
        s_own = pl.pallas_call(
            right_kernel,
            out_shape=shape(PARTS * SLOT, 128),
            scratch_shapes=[pltpu.VMEM((RANK, 128), F32)],
            compiler_params=params(),
        )(p, *arranged)
    with jax.named_scope("right_scatter"):
        s_parts = lax.all_to_all(s_own, ("rep", "tensor"), 0, 0, tiled=True)
    with jax.named_scope("right_sum"):
        s_sum, s_piece = pl.pallas_call(
            sum_right_kernel,
            out_shape=[shape(PARTS * SLOT, 128), shape(SLOT, 128)],
            compiler_params=params(),
        )(s_parts)
    with jax.named_scope("right_owner"):
        own = lax.ppermute(
            s_piece, ("rep", "col"), [(s, REPLICAS * (s % 16) + s // 16) for s in range(PARTS)]
        )
    with jax.named_scope("right_gather"):
        s = lax.all_to_all(s_sum, ("rep", "tensor"), 0, 0, tiled=True)
    with jax.named_scope("new_error"):
        return pl.pallas_call(
            error_kernel,
            out_shape=[shape(rows, cols), shape(OWN, RANK)],
            scratch_shapes=[pltpu.VMEM((RANK, 128), F32), pltpu.VMEM((cols, RANK), F32)],
            compiler_params=params(),
        )(grad, error, p, s, own)


def solution(mesh):
    n_dp, n_tensor = mesh.devices.shape
    fine = Mesh(mesh.devices.reshape(REPLICAS, n_dp // REPLICAS, n_tensor), ("rep", "col", "tensor"))
    return jax.shard_map(
        shards,
        mesh=fine,
        in_specs=(P("tensor", ("rep", "col")), P("tensor", ("rep", "col")), P()),
        out_specs=(P("tensor", ("rep", "col")), P(("rep", "col", "tensor"), None)),
        check_vma=False,
    )
```

time: 2400 us -> 93.1 us (0.04)
  blocking collectives: 1370 us -> 46.9 us
  starting transfers between devices: 596 us -> 9.53 us
  waiting for transfers between devices: 284 us -> 20.4 us
  local copies, waits for them, and re-layouts: 102 us -> 6.71 us
    unnamed x1 -> x0, blocking collectives: 1320 us -> none
    unnamed x64 -> x0, starting transfers between devices: 596 us -> none
    psum x1 -> x0, waiting for transfers between devices: 153 us -> none  [shards(): p_mean = lax.psum(p_own, 'dp') / REPLICAS]
    all_gather x1 -> x0, waiting for transfers between devices: 126 us -> none  [shards(): whole_q = lax.all_gather(q_new, ('dp', 'tensor'), axis=0, tiled=True)]
    unnamed x87 -> x7, local copies, waits for them, and re-layouts: 98.7 us -> 6.71 us
    psum x1 -> x0, blocking collectives: 47.9 us -> none  [shards(): gram = lax.psum(jnp.dot(p_mean.T, p_mean, precision=highest), 'tensor')]
    all_to_all x0 -> x2, blocking collectives: none -> 46.9 us  [the longest x1 27.7 us: shards(): s_parts = lax.all_to_all(s_own, ('rep', 'tensor'), 0, 0, tiled=True)]
  transfers between devices with their start and end apart: 66 -> 3, of which waited for: 3 -> 2; matrix products, arithmetic and copies ran while one was open for 0% -> 0% of each run, Pallas kernels for 0% -> 1%
where the time goes in v1:
time: 93.1 us; the launch traced here: 92.6 us
  blocking collectives  46.9 us (50%)
  waiting for transfers between devices  20.4 us (22%)
  starting transfers between devices  9.53 us (10%)
  Pallas kernels  8.38 us (9%)
  local copies, waits for them, and re-layouts  6.71 us (7%)
    all_to_all x1, blocking collectives, shards(): s_parts = lax.all_to_all(s_own, ('rep', 'tensor'), 0, 0, tiled=True)  27.7 us
    all_to_all x1, blocking collectives, shards(): p_parts = lax.all_to_all(p_own, ('rep', 'col'), 0, 0, tiled=True)  19.2 us
    all_to_all x1, waiting for transfers between devices, shards(): s = lax.all_to_all(s_sum, ('rep', 'tensor'), 0, 0, tiled=True)  12.9 us
    all_to_all x1, waiting for transfers between devices, shards(): p = lax.all_to_all(p_sum, ('rep', 'col'), 0, 0, tiled=True)  7.55 us
    unnamed x7, local copies, waits for them, and re-layouts  6.71 us
    all_to_all x1, starting transfers between devices, shards(): s = lax.all_to_all(s_sum, ('rep', 'tensor'), 0, 0, tiled=True)  5.02 us
    pallas_call x1, Pallas kernels, shards(): pl.pallas_call(error_kernel, out_shape=[shape(rows, cols), shape(OWN, RAN...  4.65 us
    all_to_all x1, starting transfers between devices, shards(): p = lax.all_to_all(p_sum, ('rep', 'col'), 0, 0, tiled=True)  3.86 us
  transfers between devices with their start and end apart: 3, of which 2 were waited for; matrix products, arithmetic and copies ran while one was open for 0% of the time, Pallas kernels for 1%

profile of v1, /device:TPU:1, one launch (start us, length us, event | category | flops | bytes accessed | tf_op | source)
XLA Modules:
  0.0 92.6 jit_solution(7984618041030581418)
XLA Ops:
  0.6 0.0 copy-start.2
  0.6 0.0 copy-start.1
  0.7 4.7 %copy.5.q_ref = bf16[14336,64]{1,0:T(8,128)(2,1)} copy(bf16[14336,64]{0,1:T(8,128)(2,1)} %param.5) | data formatting | bytes 3670016 | tf_op args[2]
  5.3 0.0 copy-done.2
  5.3 0.0 copy-done.1
  5.3 0.0 copy-start
  5.3 2.0 %copy-done = bf16[14336,64]{1,0:T(8,128)(2,1)S(1)} copy-done((bf16[14336,64]{1,0:T(8,128)(2,1)S(1)}, bf16[14336,64]{1,0:T(8,128)(2,1)}, u32[]{:S(2)}) %copy-start) | copy-done | bytes 1835032
  7.4 0.5 left.1
  7.9 19.2 %all_to_all.44 = f32[32,4,128]{2,1,0:T(4,128)S(1)} all-to-all(f32[32,4,128]{2,1,0:T(4,128)S(1)} %bitcast.14), channel_id=1, replica_groups=mesh['rep'=2,'col'=16,'tensor'=16] {'rep','col'}, dimensions={0} | all-to-all | bytes 131072 | tf_op jit(solution)/shard_map/left_scatter/all_to_all | solution.py:181
  27.0 0.7 left_sum.1
  27.7 3.9 %all-to-all-start.1 = ((f32[32,4,128]{2,1,0:T(4,128)}), f32[32,4,128]{2,1,0:T(4,128)S(1)}, u32[]{:S(2)}, u32[]{:S(2)}) async-start(f32[32,4,128]{2,1,0:T(4,128)} %bitcast.3), calls=%async_computation.1 | async-start | bytes 131072 | tf_op jit(solution)/shard_map/left_gather/all_to_all | solution.py:192
  31.5 1.3 %arrange.1 = (bf16[512,256]{1,0:T(8,128)(2,1)S(1)}, bf16[512,256]{1,0:T(8,128)(2,1)S(1)}, bf16[512,256]{1,0:T(8,128)(2,1)S(1)}, bf16[512,256]{1,0:T(8,128)(2,1)S(1)}) custom-call(bf16[256,896]{1,0:T(8,128)(2,1)S(1)} %copy-done.2, f32[256,896]{1,0:T(8,128)S(1)} %copy-done.1), custom_call_target="tpu_custom_call" | custom-call | flops 939524096 | bytes 2500000 | tf_op jit(solution)/shard_map/arrange/pallas_call | solution.py:183
  32.8 7.6 %all-to-all-done.1 = f32[32,4,128]{2,1,0:T(4,128)S(1)} async-done(((f32[32,4,128]{2,1,0:T(4,128)}), f32[32,4,128]{2,1,0:T(4,128)S(1)}, u32[]{:S(2)}, u32[]{:S(2)}) %all-to-all-start.1) | async-done | bytes 65568 | tf_op jit(solution)/shard_map/left_gather/all_to_all | solution.py:192
  40.4 0.5 right.1
  40.9 27.7 %all_to_all.45 = f32[32,16,128]{2,1,0:T(8,128)S(1)} all-to-all(f32[32,16,128]{2,1,0:T(8,128)S(1)} %bitcast.11), channel_id=1, replica_groups=mesh['rep'=2,'col'=16,'tensor'=16] {'rep','tensor'}, dimensions={0} | all-to-all | bytes 524288 | tf_op jit(solution)/shard_map/right_scatter/all_to_all | solution.py:201
  68.7 0.8 right_sum.1
  69.4 5.0 %all-to-all-start.3 = ((f32[32,16,128]{2,1,0:T(8,128)}), f32[32,16,128]{2,1,0:T(8,128)S(1)}, u32[]{:S(2)}, u32[]{:S(2)}) async-start(f32[32,16,128]{2,1,0:T(8,128)} %bitcast.7), calls=%async_computation.3 | async-start | bytes 524288 | tf_op jit(solution)/shard_map/right_gather/all_to_all | solution.py:213
  74.4 0.7 collective-permute-start
  75.1 0.0 collective-permute-done.own_ref
  75.1 12.9 %all-to-all-done.3 = f32[32,16,128]{2,1,0:T(8,128)S(1)} async-done(((f32[32,16,128]{2,1,0:T(8,128)}), f32[32,16,128]{2,1,0:T(8,128)S(1)}, u32[]{:S(2)}, u32[]{:S(2)}) %all-to-all-start.3) | async-done | bytes 262176 | tf_op jit(solution)/shard_map/right_gather/all_to_all | solution.py:213
  88.0 4.6 %new_error.1 = (f32[256,896]{1,0:T(8,128)}, f32[28,64]{1,0:T(8,128)}) custom-call(bf16[256,896]{1,0:T(8,128)(2,1)S(1)} %copy-done.2, f32[256,896]{1,0:T(8,128)S(1)} %copy-done.1, f32[128,128]{1,0:T(8,128)S(1)} %bitcast.13, f32[512,128]{1,0:T(8,128)S(1)} %bitcast.10, f32[16,128]{1,0:T(8,128)S(1)} %collective-permute-done.own_ref), custom_call_target="tpu_custom_call" | custom-call | tf_op jit(solution)/shard_map/new_error/pallas_call | solution.py:215
Async XLA Ops:
  0.6 4.7 %copy-start.2 = (bf16[256,896]{1,0:T(8,128)(2,1)S(1)}, bf16[256,896]{1,0:T(8,128)(2,1)}, u32[]{:S(2)}) copy-start(bf16[256,896]{1,0:T(8,128)(2,1)} %grad_ref.5) | copy-start | bytes 1376260
  0.6 4.7 %copy-start.1 = (f32[256,896]{1,0:T(8,128)S(1)}, f32[256,896]{1,0:T(8,128)}, u32[]{:S(2)}) copy-start(f32[256,896]{1,0:T(8,128)} %error_ref.5) | copy-start | bytes 2752516
  5.3 2.0 %copy-start = (bf16[14336,64]{1,0:T(8,128)(2,1)S(1)}, bf16[14336,64]{1,0:T(8,128)(2,1)}, u32[]{:S(2)}) copy-start(bf16[14336,64]{1,0:T(8,128)(2,1)} %copy.5.q_ref) | copy-start | bytes 5505028
  27.7 12.7 %all-to-all-start.1 = ((f32[32,4,128]{2,1,0:T(4,128)}), f32[32,4,128]{2,1,0:T(4,128)S(1)}, u32[]{:S(2)}, u32[]{:S(2)}) async-start(f32[32,4,128]{2,1,0:T(4,128)} %bitcast.3), calls=%async_computation.1 | async-start | bytes 131072 | tf_op jit(solution)/shard_map/left_gather/all_to_all | solution.py:192
  69.4 18.6 %all-to-all-start.3 = ((f32[32,16,128]{2,1,0:T(8,128)}), f32[32,16,128]{2,1,0:T(8,128)S(1)}, u32[]{:S(2)}, u32[]{:S(2)}) async-start(f32[32,16,128]{2,1,0:T(8,128)} %bitcast.7), calls=%async_computation.3 | async-start | bytes 524288 | tf_op jit(solution)/shard_map/right_gather/all_to_all | solution.py:213
  74.4 0.7 collective-permute-start

commit v2 on v1

--- a/solution.py
+++ b/solution.py
@@ -9,6 +9,9 @@
 RANK = 64
 PARTS = 32
 OWN = 28
+CHUNKS = 4
+LEFT_LIMIT = 62
+WIDTH = 8
 SLOT = 16
 NT = (((1,), (1,)), ((), ()))
 NN = (((1,), (0,)), ((), ()))
@@ -31,11 +34,33 @@
     return dot(a_high, b_high, dims) + (dot(a_high, b_low, dims) + dot(a_low, b_high, dims))
 
 
-def left_kernel(col_ref, grad_ref, error_ref, q_ref, out_ref):
-    high, low = split(grad_ref[...].astype(F32) + error_ref[...])
-    q = q_ref[...]
-    p = dot(high, q, NN) + dot(low, q, NN)
-    half = p.shape[0] // 2
+def left_kernel(col_ref, grad_ref, error_ref, q_ref, out_ref, grad_own, error_own, q_own, sems):
+    rows, cols = grad_own.shape
+    step = rows // CHUNKS
+    start = pl.multiple_of(col_ref[0] * cols, 128)
+    q_copy = pltpu.make_async_copy(q_ref.at[:, pl.ds(start, cols)], q_own, sems.at[0])
+    q_copy.start()
+    copies = []
+    for i in range(CHUNKS):
+        part = pl.ds(i * step, step)
+        copies.append((
+            pltpu.make_async_copy(error_ref.at[part], error_own.at[part], sems.at[1 + 2 * i]),
+            pltpu.make_async_copy(grad_ref.at[part], grad_own.at[part], sems.at[2 + 2 * i]),
+        ))
+        for copy in copies[i]:
+            copy.start()
+    q_copy.wait()
+    q = q_own[...]
+    parts = []
+    for i in range(CHUNKS):
+        for copy in copies[i]:
+            copy.wait()
+        part = slice(i * step, (i + 1) * step)
+        merged = grad_own[part].astype(F32) + error_own[part]
+        high, low = split(merged)
+        parts.append(dot(high, q, NT) + dot(low, q, NT))
+    p = jnp.concatenate(parts, axis=0)
+    half = rows // 2
     out_ref[...] = jnp.concatenate([p[:half], p[half:]], axis=1)
 
 
@@ -96,30 +121,30 @@
 def eliminate(tiles):
     sub = lax.broadcasted_iota(jnp.int32, (8, 128), 0)
     spread = lambda value: jnp.broadcast_to(value, (8, 128))
+    at = lambda values, index: spread(values[index // 8][index % 8 : index % 8 + 1, :])
     scales = [jnp.zeros((8, 128), F32) for _ in tiles]
     count = len(tiles)
-    width = 4
-    for start in range(0, RANK, width):
-        t = start // 8
-        offset = start % 8
+    for start in range(0, RANK, WIDTH):
+        begin = start // 8
         cols = [
-            {i: spread(tiles[i][:, RANK + start + q : RANK + start + q + 1]) for i in range(t, count)}
-            for q in range(width)
+            {i: spread(tiles[i][:, RANK + start + q : RANK + start + q + 1]) for i in range(begin, count)}
+            for q in range(WIDTH)
         ]
-        rows = [spread(tiles[t][offset + q : offset + q + 1, :]) for q in range(width)]
-        for q in range(width):
-            row = offset + q
-            pivot = spread(cols[q][t][row : row + 1, :])
+        rows = [at(tiles, start + q) for q in range(WIDTH)]
+        for q in range(WIDTH):
+            pivot_row = start + q
+            t = pivot_row // 8
+            pivot = at(cols[q], pivot_row)
             inverse = 1.0 / pivot
             root = lax.rsqrt(pivot)
             root = root * (1.5 - 0.5 * pivot * root * root)
-            scales[t] = jnp.where(sub == row, root, scales[t])
+            scales[t] = jnp.where(sub == pivot_row % 8, root, scales[t])
             scaled = rows[q] * inverse
-            factor = dict(cols[q])
-            factor[t] = jnp.where(sub > row, cols[q][t], 0.0)
-            for q2 in range(q + 1, width):
-                entry = spread(cols[q2][t][row : row + 1, :]) * inverse
-                rows[q2] = rows[q2] - spread(factor[t][offset + q2 : offset + q2 + 1, :]) * scaled
+            factor = {i: cols[q][i] for i in range(t, count)}
+            factor[t] = jnp.where(sub > pivot_row % 8, cols[q][t], 0.0)
+            for q2 in range(q + 1, WIDTH):
+                entry = at(cols[q2], pivot_row) * inverse
+                rows[q2] = rows[q2] - at(factor, start + q2) * scaled
                 for i in range(t, count):
                     cols[q2][i] = cols[q2][i] - factor[i] * entry
             for i in range(t, count):
@@ -127,7 +152,8 @@
     return [tile * scale for tile, scale in zip(tiles, scales)]
 
 
-def error_kernel(grad_ref, error_ref, p_ref, s_ref, own_ref, error_out_ref, q_out_ref, table_ref, right_ref):
+def error_kernel(grad_ref, error_ref, p_ref, s_ref, own_ref, error_out_ref, q_out_ref, table_ref, right_ref, result_ref, sems):
+    rows, cols = error_ref.shape
     row = lax.broadcasted_iota(jnp.int32, (RANK, 128), 0)
     lane = lax.broadcasted_iota(jnp.int32, (RANK, 128), 1)
     table_ref[...] = (row == lane).astype(F32)
@@ -137,55 +163,79 @@
     inverse = jnp.where(lane < RANK, jnp.concatenate(tiles, axis=0), 0.0)
     both = jnp.concatenate([inverse, pltpu.roll(inverse, RANK, 1)], axis=0)
     basis = dot3(p_ref[...], both, NT)
-    basis = jnp.concatenate([basis[:, :RANK], basis[:, RANK:]], axis=0)
+    turned = pltpu.roll(basis, RANK, 1)
+    lower = lax.broadcasted_iota(jnp.int32, basis.shape, 1) < RANK
+    whole = jnp.concatenate([jnp.where(lower, basis, turned), jnp.where(lower, turned, basis)], axis=0)
+    high = whole.astype(BF16)
+    low = jnp.where(jnp.concatenate([lower, lower], axis=0), whole - high.astype(F32), 0.0)
+    left = jnp.concatenate([high, low.astype(BF16)], axis=0)
     right = 0.5 * dot3(s_ref[...], both, NT)
-    shifted = pltpu.roll(right, RANK, 1)
+    high = right.astype(BF16).astype(F32)
+    low = right - high
+    lower = lax.broadcasted_iota(jnp.int32, right.shape, 1) < RANK
+    first = jnp.where(lower, high, pltpu.roll(low, RANK, 1))
+    last = jnp.where(lower, pltpu.roll(high, RANK, 1), low)
     for k in range(PARTS):
-        right_ref[OWN * k : OWN * k + SLOT, :] = right[SLOT * k : SLOT * k + SLOT, :RANK]
-        right_ref[OWN * k + SLOT : OWN * k + OWN, :] = shifted[SLOT * k : SLOT * k + OWN - SLOT, :RANK]
+        right_ref[OWN * k : OWN * k + SLOT, :] = first[SLOT * k : SLOT * k + SLOT]
+        right_ref[OWN * k + SLOT : OWN * k + OWN, :] = last[SLOT * k : SLOT * k + OWN - SLOT]
+    copies = []
+    for i in range(0, cols, 256):
+        width = min(256, cols - i)
+        products = dot(left, right_ref[i : i + width, :].astype(BF16), NT)
+        merged = grad_ref[:, i : i + width].astype(F32) + error_ref[:, i : i + width]
+        result_ref[:, i : i + width] = merged - (products[:rows] + products[rows:])
+        part = pl.ds(i, width)
+        copies.append(pltpu.make_async_copy(result_ref.at[:, part], error_out_ref.at[:, part], sems.at[i // 256]))
+        copies[-1].start()
     own = 0.5 * dot3(own_ref[...], both, NT)
     q_out_ref[:SLOT, :] = own[:, :RANK]
     q_out_ref[SLOT:, :] = pltpu.roll(own, RANK, 1)[: OWN - SLOT, :RANK]
-    merged = grad_ref[...].astype(F32) + error_ref[...]
-    error_out_ref[...] = merged - dot3(basis, right_ref[...], NT)
+    for copy in copies:
+        copy.wait()
 
 
 def shape(*dims, kind=F32):
     return jax.ShapeDtypeStruct(dims, kind)
 
 
-def params():
-    return pltpu.CompilerParams(vmem_limit_bytes=24 * 1024 * 1024)
+def params(limit=24):
+    return pltpu.CompilerParams(vmem_limit_bytes=limit * 1024 * 1024)
+
+
+def cost(flops, moved):
+    return pl.CostEstimate(flops=flops, bytes_accessed=moved, transcendentals=0)
 
 
 def shards(grad, error, q_start):
     rows, cols = grad.shape
     col = lax.axis_index("col").astype(jnp.int32).reshape(1)
+    hbm = pl.BlockSpec(memory_space=pltpu.HBM)
+    vmem = pl.BlockSpec(memory_space=pltpu.VMEM)
+    smem = pl.BlockSpec(memory_space=pltpu.SMEM)
     with jax.named_scope("left"):
         p_own = pl.pallas_call(
             left_kernel,
-            grid_spec=pltpu.PrefetchScalarGridSpec(
-                num_scalar_prefetch=1,
-                grid=(1,),
-                in_specs=[
-                    pl.BlockSpec((rows, cols), lambda i, c: (0, 0)),
-                    pl.BlockSpec((rows, cols), lambda i, c: (0, 0)),
-                    pl.BlockSpec((cols, RANK), lambda i, c: (c[0], 0)),
-                ],
-                out_specs=pl.BlockSpec((rows // 2, 128), lambda i, c: (0, 0)),
-            ),
+            in_specs=[smem, hbm, hbm, hbm],
+            out_specs=vmem,
             out_shape=shape(rows // 2, 128),
-            compiler_params=params(),
-        )(col, grad, error, q_start)
-    with jax.named_scope("left_scatter"):
-        p_parts = lax.all_to_all(p_own, ("rep", "col"), 0, 0, tiled=True)
+            scratch_shapes=[
+                pltpu.VMEM((rows, cols), BF16),
+                pltpu.VMEM((rows, cols), F32),
+                pltpu.VMEM((RANK, cols), BF16),
+                pltpu.SemaphoreType.DMA((1 + 2 * CHUNKS,)),
+            ],
+            compiler_params=params(LEFT_LIMIT),
+        )(col, grad, error, q_start.T)
     with jax.named_scope("arrange"):
+        p_own, grad, error = lax.optimization_barrier((p_own, grad, error))
         arranged = pl.pallas_call(
             arrange_kernel,
             out_shape=[shape(PARTS * SLOT, rows, kind=BF16)] * 4,
             compiler_params=params(),
-            cost_estimate=pl.CostEstimate(flops=2 * 4 * 512 * 256 * 896, bytes_accessed=2500000, transcendentals=0),
+            cost_estimate=cost(2 * 4 * 512 * 256 * 896, 2500000),
         )(grad, error)
+    with jax.named_scope("left_scatter"):
+        p_parts = lax.all_to_all(p_own, ("rep", "col"), 0, 0, tiled=True)
     with jax.named_scope("left_sum"):
         p_sum = pl.pallas_call(sum_left_kernel, out_shape=shape(rows // 2, 128), compiler_params=params())(p_parts)
     with jax.named_scope("left_gather"):
@@ -214,8 +264,14 @@
     with jax.named_scope("new_error"):
         return pl.pallas_call(
             error_kernel,
+            out_specs=[hbm, vmem],
             out_shape=[shape(rows, cols), shape(OWN, RANK)],
-            scratch_shapes=[pltpu.VMEM((RANK, 128), F32), pltpu.VMEM((cols, RANK), F32)],
+            scratch_shapes=[
+                pltpu.VMEM((RANK, 128), F32),
+                pltpu.VMEM((cols, 128), F32),
+                pltpu.VMEM((rows, cols), F32),
+                pltpu.SemaphoreType.DMA((-(-cols // 256),)),
+            ],
             compiler_params=params(),
         )(grad, error, p, s, own)
 
@@ -223,10 +279,11 @@
 def solution(mesh):
     n_dp, n_tensor = mesh.devices.shape
     fine = Mesh(mesh.devices.reshape(REPLICAS, n_dp // REPLICAS, n_tensor), ("rep", "col", "tensor"))
+    blocks = P("tensor", ("rep", "col"))
     return jax.shard_map(
         shards,
         mesh=fine,
-        in_specs=(P("tensor", ("rep", "col")), P("tensor", ("rep", "col")), P()),
-        out_specs=(P("tensor", ("rep", "col")), P(("rep", "col", "tensor"), None)),
+        in_specs=(blocks, blocks, P()),
+        out_specs=(blocks, P(("rep", "col", "tensor"), None)),
         check_vma=False,
     )

time: 93.1 us -> 88.3 us (0.948)
  local copies, waits for them, and re-layouts: 6.71 us -> 0.01 us
  Pallas kernels: 8.38 us -> 10.1 us
    unnamed x7 -> x4, local copies, waits for them, and re-layouts: 6.71 us -> 0.01 us
    pallas_call x2, Pallas kernels: 5.13 us -> 6.9 us  [the longest x1 4.07 us: shards(): pl.pallas_call(error_kernel, out_specs=[hbm, vmem], out_shape=[shape(rows...]
where the time goes in v2:
time: 88.3 us; the launch traced here: 87.9 us
  blocking collectives  47.1 us (53%)
  waiting for transfers between devices  20.4 us (23%)
  Pallas kernels  10.1 us (11%)
  starting transfers between devices  9.53 us (11%)
    all_to_all x1, blocking collectives, shards(): s_parts = lax.all_to_all(s_own, ('rep', 'tensor'), 0, 0, tiled=True)  27.7 us
    all_to_all x1, blocking collectives, shards(): p_parts = lax.all_to_all(p_own, ('rep', 'col'), 0, 0, tiled=True)  19.4 us
    all_to_all x1, waiting for transfers between devices, shards(): s = lax.all_to_all(s_sum, ('rep', 'tensor'), 0, 0, tiled=True)  12.9 us
    all_to_all x1, waiting for transfers between devices, shards(): p = lax.all_to_all(p_sum, ('rep', 'col'), 0, 0, tiled=True)  7.54 us
    all_to_all x1, starting transfers between devices, shards(): s = lax.all_to_all(s_sum, ('rep', 'tensor'), 0, 0, tiled=True)  5.02 us
    pallas_call x1, Pallas kernels, shards(): pl.pallas_call(error_kernel, out_specs=[hbm, vmem], out_shape=[shape(rows...  4.07 us
    all_to_all x1, starting transfers between devices, shards(): p = lax.all_to_all(p_sum, ('rep', 'col'), 0, 0, tiled=True)  3.85 us
    pallas_call x1, Pallas kernels, shards(): pl.pallas_call(left_kernel, in_specs=[smem, hbm, hbm, hbm], out_specs=vme...  2.83 us
  transfers between devices with their start and end apart: 3, of which 2 were waited for; matrix products, arithmetic and copies ran while one was open for 0% of the time, Pallas kernels for 1%

profile of v2, /device:TPU:1, one launch (start us, length us, event | category | flops | bytes accessed | tf_op | source)
XLA Modules:
  0.0 87.9 jit_solution(11384709789114739071)
XLA Ops:
  0.6 0.0 copy-start
  0.6 0.0 copy-start.1
  0.7 2.8 %left.1 = f32[128,128]{1,0:T(8,128)} custom-call(s32[1]{0:T(128)} %bitcast.col_ref, bf16[256,896]{1,0:T(8,128)(2,1)} %grad_ref.3, f32[256,896]{1,0:T(8,128)} %error_ref.3, bf16[64,14336]{1,0:T(8,128)(2,1)} %bitcast.16), custom_call_target="tpu_custom_call" | custom-call | tf_op jit(solution)/shard_map/left/pallas_call | solution.py:216
  3.5 19.4 %all_to_all.44 = f32[32,4,128]{2,1,0:T(4,128)S(1)} all-to-all(f32[32,4,128]{2,1,0:T(4,128)} %bitcast.17), channel_id=1, replica_groups=mesh['rep'=2,'col'=16,'tensor'=16] {'rep','col'}, dimensions={0} | all-to-all | bytes 131072 | tf_op jit(solution)/shard_map/left_scatter/all_to_all | solution.py:238
  22.9 0.7 left_sum.1
  23.5 3.9 %all-to-all-start.1 = ((f32[32,4,128]{2,1,0:T(4,128)}), f32[32,4,128]{2,1,0:T(4,128)S(1)}, u32[]{:S(2)}, u32[]{:S(2)}) async-start(f32[32,4,128]{2,1,0:T(4,128)} %bitcast.4), calls=%async_computation.1 | async-start | bytes 131072 | tf_op jit(solution)/shard_map/left_gather/all_to_all | solution.py:242
  27.4 0.0 copy-done
  27.4 0.0 copy-done.1
  27.4 1.3 %arrange.1 = (bf16[512,256]{1,0:T(8,128)(2,1)S(1)}, bf16[512,256]{1,0:T(8,128)(2,1)S(1)}, bf16[512,256]{1,0:T(8,128)(2,1)S(1)}, bf16[512,256]{1,0:T(8,128)(2,1)S(1)}) custom-call(bf16[256,896]{1,0:T(8,128)(2,1)S(1)} %copy-done.1, f32[256,896]{1,0:T(8,128)S(1)} %copy-done), custom_call_target="tpu_custom_call" | custom-call | flops 939524096 | bytes 2500000 | tf_op jit(solution)/shard_map/arrange/pallas_call | solution.py:231
  28.7 7.5 %all-to-all-done.1 = f32[32,4,128]{2,1,0:T(4,128)S(1)} async-done(((f32[32,4,128]{2,1,0:T(4,128)}), f32[32,4,128]{2,1,0:T(4,128)S(1)}, u32[]{:S(2)}, u32[]{:S(2)}) %all-to-all-start.1) | async-done | bytes 65568 | tf_op jit(solution)/shard_map/left_gather/all_to_all | solution.py:242
  36.2 0.5 right.1
  36.8 27.7 %all_to_all.45 = f32[32,16,128]{2,1,0:T(8,128)S(1)} all-to-all(f32[32,16,128]{2,1,0:T(8,128)S(1)} %bitcast.12), channel_id=1, replica_groups=mesh['rep'=2,'col'=16,'tensor'=16] {'rep','tensor'}, dimensions={0} | all-to-all | bytes 524288 | tf_op jit(solution)/shard_map/right_scatter/all_to_all | solution.py:251
  64.5 0.8 right_sum.1
  65.3 5.0 %all-to-all-start.3 = ((f32[32,16,128]{2,1,0:T(8,128)}), f32[32,16,128]{2,1,0:T(8,128)S(1)}, u32[]{:S(2)}, u32[]{:S(2)}) async-start(f32[32,16,128]{2,1,0:T(8,128)} %bitcast.8), calls=%async_computation.3 | async-start | bytes 524288 | tf_op jit(solution)/shard_map/right_gather/all_to_all | solution.py:263
  70.3 0.7 collective-permute-start
  71.0 0.0 collective-permute-done.own_ref
  71.0 12.9 %all-to-all-done.3 = f32[32,16,128]{2,1,0:T(8,128)S(1)} async-done(((f32[32,16,128]{2,1,0:T(8,128)}), f32[32,16,128]{2,1,0:T(8,128)S(1)}, u32[]{:S(2)}, u32[]{:S(2)}) %all-to-all-start.3) | async-done | bytes 262176 | tf_op jit(solution)/shard_map/right_gather/all_to_all | solution.py:263
  83.8 4.1 %new_error.1 = (f32[256,896]{1,0:T(8,128)}, f32[28,64]{1,0:T(8,128)}) custom-call(bf16[256,896]{1,0:T(8,128)(2,1)S(1)} %copy-done.1, f32[256,896]{1,0:T(8,128)S(1)} %copy-done, f32[128,128]{1,0:T(8,128)S(1)} %bitcast.14, f32[512,128]{1,0:T(8,128)S(1)} %bitcast.11, f32[16,128]{1,0:T(8,128)S(1)} %collective-permute-done.own_ref), custom_call_target="tpu_custom_call" | custom-call | tf_op jit(solution)/shard_map/new_error/pallas_call | solution.py:265
Async XLA Ops:
  0.6 26.7 %copy-start = (f32[256,896]{1,0:T(8,128)S(1)}, f32[256,896]{1,0:T(8,128)}, u32[]{:S(2)}) copy-start(f32[256,896]{1,0:T(8,128)} %error_ref.3) | copy-start | bytes 2752516
  0.6 26.7 %copy-start.1 = (bf16[256,896]{1,0:T(8,128)(2,1)S(1)}, bf16[256,896]{1,0:T(8,128)(2,1)}, u32[]{:S(2)}) copy-start(bf16[256,896]{1,0:T(8,128)(2,1)} %grad_ref.3) | copy-start | bytes 1376260
  23.5 12.7 %all-to-all-start.1 = ((f32[32,4,128]{2,1,0:T(4,128)}), f32[32,4,128]{2,1,0:T(4,128)S(1)}, u32[]{:S(2)}, u32[]{:S(2)}) async-start(f32[32,4,128]{2,1,0:T(4,128)} %bitcast.4), calls=%async_computation.1 | async-start | bytes 131072 | tf_op jit(solution)/shard_map/left_gather/all_to_all | solution.py:242
  65.3 18.6 %all-to-all-start.3 = ((f32[32,16,128]{2,1,0:T(8,128)}), f32[32,16,128]{2,1,0:T(8,128)S(1)}, u32[]{:S(2)}, u32[]{:S(2)}) async-start(f32[32,16,128]{2,1,0:T(8,128)} %bitcast.8), calls=%async_computation.3 | async-start | bytes 524288 | tf_op jit(solution)/shard_map/right_gather/all_to_all | solution.py:263
  70.3 0.7 collective-permute-start

commit v3 on v2

--- a/solution.py
+++ b/solution.py
@@ -9,8 +9,11 @@
 RANK = 64
 PARTS = 32
 OWN = 28
-CHUNKS = 4
-LEFT_LIMIT = 62
+CORES = 2
+HALF = PARTS // CORES
+CHUNKS = 2
+LEFT_LIMIT = 54912
+PAYLOAD = 256
 WIDTH = 8
 SLOT = 16
 NT = (((1,), (1,)), ((), ()))
@@ -109,13 +112,14 @@
     turned = jnp.concatenate([turned[:RANK], turned[RANK:]], axis=1)
     gram_ref[...] = dot3(turned, right, NN)
     for k in range(PARTS):
-        out_ref[SLOT * k + 12 : SLOT * k + 14, RANK:] = gram_ref[2 * k : 2 * k + 2, RANK:]
+        first = 4 * (k // CORES)
+        out_ref[SLOT * k + 12 : SLOT * k + 16, RANK:] = gram_ref[first : first + 4, RANK:]
 
 
 def sum_right_kernel(in_ref, out_ref, own_ref):
     total = jnp.sum(in_ref[...].reshape(PARTS, SLOT, 128), axis=0)
-    own_ref[...] = total
-    out_ref[...] = jnp.broadcast_to(total[None], (PARTS, SLOT, 128)).reshape(PARTS * SLOT, 128)
+    own_ref[...] = jnp.broadcast_to(total[None], (PAYLOAD // SLOT, SLOT, 128)).reshape(PAYLOAD, 128)
+    out_ref[...] = jnp.broadcast_to(total[None], (HALF, SLOT, 128)).reshape(HALF * SLOT, 128)
 
 
 def eliminate(tiles):
@@ -152,44 +156,61 @@
     return [tile * scale for tile, scale in zip(tiles, scales)]
 
 
-def error_kernel(grad_ref, error_ref, p_ref, s_ref, own_ref, error_out_ref, q_out_ref, table_ref, right_ref, result_ref, sems):
-    rows, cols = error_ref.shape
+def basis_kernel(p_ref, s_ref, inverse_ref, basis_ref, table_ref):
     row = lax.broadcasted_iota(jnp.int32, (RANK, 128), 0)
     lane = lax.broadcasted_iota(jnp.int32, (RANK, 128), 1)
     table_ref[...] = (row == lane).astype(F32)
-    for k in range(PARTS):
-        table_ref[2 * k : 2 * k + 2, RANK:] = 0.5 * s_ref[SLOT * k + 12 : SLOT * k + 14, RANK:]
+    for h in range(HALF):
+        table_ref[4 * h : 4 * h + 4, RANK:] = 0.5 * s_ref[SLOT * h + 12 : SLOT * h + 16, RANK:]
     tiles = eliminate([table_ref[8 * i : 8 * i + 8, :] for i in range(RANK // 8)])
     inverse = jnp.where(lane < RANK, jnp.concatenate(tiles, axis=0), 0.0)
-    both = jnp.concatenate([inverse, pltpu.roll(inverse, RANK, 1)], axis=0)
-    basis = dot3(p_ref[...], both, NT)
+    turned = pltpu.roll(inverse, RANK, 1)
+    high, low = split(inverse)
+    inverse_ref[...] = jnp.concatenate([split(inverse + turned)[0], low], axis=0)
+    basis = dot3(p_ref[...], jnp.concatenate([inverse, turned], axis=0), NT)
     turned = pltpu.roll(basis, RANK, 1)
     lower = lax.broadcasted_iota(jnp.int32, basis.shape, 1) < RANK
     whole = jnp.concatenate([jnp.where(lower, basis, turned), jnp.where(lower, turned, basis)], axis=0)
     high = whole.astype(BF16)
     low = jnp.where(jnp.concatenate([lower, lower], axis=0), whole - high.astype(F32), 0.0)
-    left = jnp.concatenate([high, low.astype(BF16)], axis=0)
-    right = 0.5 * dot3(s_ref[...], both, NT)
-    high = right.astype(BF16).astype(F32)
-    low = right - high
-    lower = lax.broadcasted_iota(jnp.int32, right.shape, 1) < RANK
-    first = jnp.where(lower, high, pltpu.roll(low, RANK, 1))
-    last = jnp.where(lower, pltpu.roll(high, RANK, 1), low)
-    for k in range(PARTS):
-        right_ref[OWN * k : OWN * k + SLOT, :] = first[SLOT * k : SLOT * k + SLOT]
-        right_ref[OWN * k + SLOT : OWN * k + OWN, :] = last[SLOT * k : SLOT * k + OWN - SLOT]
-    copies = []
+    basis_ref[...] = jnp.concatenate([high, low.astype(BF16)], axis=0)
+
+
+def pair(s):
+    lower = lax.broadcasted_iota(jnp.int32, s.shape, 1) < RANK
+    high = s.astype(BF16).astype(F32)
+    low = s - high
+    return jnp.where(lower, high, pltpu.roll(low, RANK, 1)), jnp.where(lower, pltpu.roll(high, RANK, 1), low)
+
+
+def error_kernel(core_ref, grad_ref, error_ref, inverse_ref, basis_ref, near_ref, far_ref, own_ref, error_out_ref, q_out_ref, right_ref, result_ref, own_out, sems):
+    rows, cols = error_ref.shape
+    inverse = inverse_ref[...]
+    near = near_ref[...]
+    far = far_ref[...]
+    swapped = core_ref[0] == 1
+    for core, s in enumerate((jnp.where(swapped, far, near), jnp.where(swapped, near, far))):
+        first, last = pair(s)
+        for h in range(HALF):
+            start = OWN * (CORES * h + core)
+            right_ref[start : start + SLOT, :] = first[SLOT * h : SLOT * h + SLOT]
+            right_ref[start + SLOT : start + OWN, :] = last[SLOT * h : SLOT * h + OWN - SLOT]
+    first, last = pair(own_ref[:SLOT])
+    own = dot(jnp.concatenate([first, last], axis=0).astype(BF16), inverse, NT)
+    own = 0.5 * (own + pltpu.roll(own, RANK, 1))
+    own_out[...] = own[:OWN, :RANK]
+    copies = [pltpu.make_async_copy(own_out, q_out_ref, sems.at[0])]
+    copies[0].start()
     for i in range(0, cols, 256):
         width = min(256, cols - i)
-        products = dot(left, right_ref[i : i + width, :].astype(BF16), NT)
+        right = dot(inverse, right_ref[i : i + width, :].astype(BF16), NT)
+        high, low = split(0.5 * (right[:RANK] + right[RANK:]))
+        products = dot(basis_ref[...], jnp.concatenate([high, low], axis=0), NN)
         merged = grad_ref[:, i : i + width].astype(F32) + error_ref[:, i : i + width]
         result_ref[:, i : i + width] = merged - (products[:rows] + products[rows:])
         part = pl.ds(i, width)
-        copies.append(pltpu.make_async_copy(result_ref.at[:, part], error_out_ref.at[:, part], sems.at[i // 256]))
+        copies.append(pltpu.make_async_copy(result_ref.at[:, part], error_out_ref.at[:, part], sems.at[1 + i // 256]))
         copies[-1].start()
-    own = 0.5 * dot3(own_ref[...], both, NT)
-    q_out_ref[:SLOT, :] = own[:, :RANK]
-    q_out_ref[SLOT:, :] = pltpu.roll(own, RANK, 1)[: OWN - SLOT, :RANK]
     for copy in copies:
         copy.wait()
 
@@ -198,8 +219,8 @@
     return jax.ShapeDtypeStruct(dims, kind)
 
 
-def params(limit=24):
-    return pltpu.CompilerParams(vmem_limit_bytes=limit * 1024 * 1024)
+def params(limit=24 * 1024):
+    return pltpu.CompilerParams(vmem_limit_bytes=limit * 1024)
 
 
 def cost(flops, moved):
@@ -209,6 +230,7 @@
 def shards(grad, error, q_start):
     rows, cols = grad.shape
     col = lax.axis_index("col").astype(jnp.int32).reshape(1)
+    core = lax.axis_index("core").astype(jnp.int32).reshape(1)
     hbm = pl.BlockSpec(memory_space=pltpu.HBM)
     vmem = pl.BlockSpec(memory_space=pltpu.VMEM)
     smem = pl.BlockSpec(memory_space=pltpu.SMEM)
@@ -248,11 +270,11 @@
             compiler_params=params(),
         )(p, *arranged)
     with jax.named_scope("right_scatter"):
-        s_parts = lax.all_to_all(s_own, ("rep", "tensor"), 0, 0, tiled=True)
+        s_parts = lax.all_to_all(s_own, ("rep", "z", "core"), 0, 0, tiled=True)
     with jax.named_scope("right_sum"):
         s_sum, s_piece = pl.pallas_call(
             sum_right_kernel,
-            out_shape=[shape(PARTS * SLOT, 128), shape(SLOT, 128)],
+            out_shape=[shape(HALF * SLOT, 128), shape(PAYLOAD, 128)],
             compiler_params=params(),
         )(s_parts)
     with jax.named_scope("right_owner"):
@@ -260,30 +282,43 @@
             s_piece, ("rep", "col"), [(s, REPLICAS * (s % 16) + s // 16) for s in range(PARTS)]
         )
     with jax.named_scope("right_gather"):
-        s = lax.all_to_all(s_sum, ("rep", "tensor"), 0, 0, tiled=True)
+        near = lax.all_to_all(s_sum, ("rep", "z"), 0, 0, tiled=True)
+    with jax.named_scope("right_swap"):
+        far = lax.ppermute(near, "core", [(0, 1), (1, 0)])
+    with jax.named_scope("basis"):
+        inverse, basis = pl.pallas_call(
+            basis_kernel,
+            out_shape=[shape(128, 128, kind=BF16), shape(2 * rows, 128, kind=BF16)],
+            scratch_shapes=[pltpu.VMEM((RANK, 128), F32)],
+            compiler_params=params(),
+            cost_estimate=cost(1000, 1000),
+        )(p, near)
     with jax.named_scope("new_error"):
         return pl.pallas_call(
             error_kernel,
-            out_specs=[hbm, vmem],
+            in_specs=[smem] + [vmem] * 7,
+            out_specs=[hbm, hbm],
             out_shape=[shape(rows, cols), shape(OWN, RANK)],
             scratch_shapes=[
-                pltpu.VMEM((RANK, 128), F32),
                 pltpu.VMEM((cols, 128), F32),
                 pltpu.VMEM((rows, cols), F32),
-                pltpu.SemaphoreType.DMA((-(-cols // 256),)),
+                pltpu.VMEM((OWN, RANK), F32),
+                pltpu.SemaphoreType.DMA((1 + -(-cols // 256),)),
             ],
             compiler_params=params(),
-        )(grad, error, p, s, own)
+            cost_estimate=cost(1000, 1000),
+        )(core, grad, error, inverse, basis, near, far, own)
 
 
 def solution(mesh):
     n_dp, n_tensor = mesh.devices.shape
-    fine = Mesh(mesh.devices.reshape(REPLICAS, n_dp // REPLICAS, n_tensor), ("rep", "col", "tensor"))
-    blocks = P("tensor", ("rep", "col"))
+    grid = mesh.devices.reshape(REPLICAS, n_dp // REPLICAS, n_tensor // CORES, CORES)
+    fine = Mesh(grid, ("rep", "col", "z", "core"))
+    blocks = P(("z", "core"), ("rep", "col"))
     return jax.shard_map(
         shards,
         mesh=fine,
         in_specs=(blocks, blocks, P()),
-        out_specs=(blocks, P(("rep", "col", "tensor"), None)),
+        out_specs=(blocks, P(("rep", "col", "z", "core"), None)),
         check_vma=False,
     )

time: 88.3 us -> 85.2 us (0.965)
  waiting for transfers between devices: 20.4 us -> 15.7 us
  starting transfers between devices: 9.53 us -> 12.6 us
  Pallas kernels: 10.1 us -> 8.85 us
    all_to_all x1, waiting for transfers between devices: 12.9 us -> 8.2 us  [shards(): near = lax.all_to_all(s_sum, ('rep', 'z'), 0, 0, tiled=True)]
    ppermute x0 -> x1, starting transfers between devices: none -> 4.54 us  [shards(): far = lax.ppermute(near, 'core', [(0, 1), (1, 0)])]
    all_to_all x1, starting transfers between devices: 5.02 us -> 3.51 us  [shards(): near = lax.all_to_all(s_sum, ('rep', 'z'), 0, 0, tiled=True)]
    pallas_call x1, Pallas kernels: 2.83 us -> 1.92 us  [shards(): pl.pallas_call(left_kernel, in_specs=[smem, hbm, hbm, hbm], out_specs=vme...]
    pallas_call x2 -> x3, Pallas kernels: 4.82 us -> 4.44 us  [the longest x1 2.09 us: shards(): pl.pallas_call(basis_kernel, out_shape=[shape(128, 128, kind=BF16), shape...]
  transfers between devices with their start and end apart: 3 -> 4, of which waited for: 2 -> 2; matrix products, arithmetic and copies ran while one was open for 0% -> 0% of each run, Pallas kernels for 1% -> 4%
where the time goes in v3:
time: 85.2 us; the launch traced here: 84.8 us
  blocking collectives  46.9 us (55%)
  waiting for transfers between devices  15.7 us (18%)
  starting transfers between devices  12.6 us (15%)
  Pallas kernels  8.85 us (10%)
    all_to_all x1, blocking collectives, shards(): s_parts = lax.all_to_all(s_own, ('rep', 'z', 'core'), 0, 0, tiled=True)  27.7 us
    all_to_all x1, blocking collectives, shards(): p_parts = lax.all_to_all(p_own, ('rep', 'col'), 0, 0, tiled=True)  19.2 us
    all_to_all x1, waiting for transfers between devices, shards(): near = lax.all_to_all(s_sum, ('rep', 'z'), 0, 0, tiled=True)  8.2 us
    all_to_all x1, waiting for transfers between devices, shards(): p = lax.all_to_all(p_sum, ('rep', 'col'), 0, 0, tiled=True)  7.53 us
    ppermute x1, starting transfers between devices, shards(): far = lax.ppermute(near, 'core', [(0, 1), (1, 0)])  4.54 us
    all_to_all x1, starting transfers between devices, shards(): p = lax.all_to_all(p_sum, ('rep', 'col'), 0, 0, tiled=True)  3.85 us
    all_to_all x1, starting transfers between devices, shards(): near = lax.all_to_all(s_sum, ('rep', 'z'), 0, 0, tiled=True)  3.51 us
    pallas_call x1, Pallas kernels, shards(): pl.pallas_call(basis_kernel, out_shape=[shape(128, 128, kind=BF16), shape...  2.09 us
  transfers between devices with their start and end apart: 4, of which 2 were waited for; matrix products, arithmetic and copies ran while one was open for 0% of the time, Pallas kernels for 4%

profile of v3, /device:TPU:1, one launch (start us, length us, event | category | flops | bytes accessed | tf_op | source)
XLA Modules:
  0.0 84.8 jit_solution(8925943383435828668)
XLA Ops:
  0.6 0.0 copy-start
  0.6 0.0 copy-start.1
  0.7 1.9 %left.1 = f32[128,128]{1,0:T(8,128)S(1)} custom-call(s32[1]{0:T(128)} %bitcast.1.col_ref, bf16[256,896]{1,0:T(8,128)(2,1)} %grad_ref.3, f32[256,896]{1,0:T(8,128)} %error_ref.3, bf16[64,14336]{1,0:T(8,128)(2,1)} %bitcast.20), custom_call_target="tpu_custom_call" | custom-call | tf_op jit(solution)/shard_map/left/pallas_call | solution.py:238
  2.6 19.2 %all_to_all.44 = f32[32,4,128]{2,1,0:T(4,128)S(1)} all-to-all(f32[32,4,128]{2,1,0:T(4,128)S(1)} %bitcast.18), channel_id=1, replica_groups=mesh['rep'=2,'col'=16,'z'=8,'core'=2] {'rep','col'}, dimensions={0} | all-to-all | bytes 131072 | tf_op jit(solution)/shard_map/left_scatter/all_to_all | solution.py:260
  21.7 0.7 left_sum.1
  22.4 3.9 %all-to-all-start.1 = ((f32[32,4,128]{2,1,0:T(4,128)}), f32[32,4,128]{2,1,0:T(4,128)S(1)}, u32[]{:S(2)}, u32[]{:S(2)}) async-start(f32[32,4,128]{2,1,0:T(4,128)} %bitcast.5), calls=%async_computation.1 | async-start | bytes 131072 | tf_op jit(solution)/shard_map/left_gather/all_to_all | solution.py:264
  26.2 0.0 copy-done
  26.3 0.0 copy-done.1
  26.3 1.3 %arrange.1 = (bf16[512,256]{1,0:T(8,128)(2,1)S(1)}, bf16[512,256]{1,0:T(8,128)(2,1)S(1)}, bf16[512,256]{1,0:T(8,128)(2,1)S(1)}, bf16[512,256]{1,0:T(8,128)(2,1)S(1)}) custom-call(bf16[256,896]{1,0:T(8,128)(2,1)S(1)} %copy-done.1, f32[256,896]{1,0:T(8,128)S(1)} %copy-done), custom_call_target="tpu_custom_call" | custom-call | flops 939524096 | bytes 2500000 | tf_op jit(solution)/shard_map/arrange/pallas_call | solution.py:253
  27.6 7.5 %all-to-all-done.1 = f32[32,4,128]{2,1,0:T(4,128)S(1)} async-done(((f32[32,4,128]{2,1,0:T(4,128)}), f32[32,4,128]{2,1,0:T(4,128)S(1)}, u32[]{:S(2)}, u32[]{:S(2)}) %all-to-all-start.1) | async-done | bytes 65568 | tf_op jit(solution)/shard_map/left_gather/all_to_all | solution.py:264
  35.1 0.5 right.1
  35.7 27.7 %all_to_all.45 = f32[32,16,128]{2,1,0:T(8,128)S(1)} all-to-all(f32[32,16,128]{2,1,0:T(8,128)S(1)} %bitcast.15), channel_id=1, replica_groups=mesh['rep'=2,'col'=16,'z'=8,'core'=2] {'rep','z','core'}, dimensions={0} | all-to-all | bytes 524288 | tf_op jit(solution)/shard_map/right_scatter/all_to_all | solution.py:273
  63.4 0.7 right_sum.1
  64.1 3.5 %all-to-all-start.3 = ((f32[16,16,128]{2,1,0:T(8,128)}), f32[16,16,128]{2,1,0:T(8,128)S(1)}, u32[]{:S(2)}, u32[]{:S(2)}) async-start(f32[16,16,128]{2,1,0:T(8,128)} %bitcast.9), calls=%async_computation.3 | async-start | bytes 262144 | tf_op jit(solution)/shard_map/right_gather/all_to_all | solution.py:285
  67.6 0.7 collective-permute-start.1
  68.3 8.2 %all-to-all-done.3 = f32[16,16,128]{2,1,0:T(8,128)S(1)} async-done(((f32[16,16,128]{2,1,0:T(8,128)}), f32[16,16,128]{2,1,0:T(8,128)S(1)}, u32[]{:S(2)}, u32[]{:S(2)}) %all-to-all-start.3) | async-done | bytes 131104 | tf_op jit(solution)/shard_map/right_gather/all_to_all | solution.py:285
  76.5 4.5 %collective-permute-start = (f32[256,128]{1,0:T(8,128)S(1)}, f32[256,128]{1,0:T(8,128)S(1)}, u32[]{:S(2)}, u32[]{:S(2)}) collective-permute-start(f32[256,128]{1,0:T(8,128)S(1)} %bitcast.11), channel_id=1, source_target_pairs={{0,1},{1,0},{2,3},{3,2},{4,5},{5,4},{6,7},{7,6},{8,9},{9,8},{10,11... | collective-permute-start | bytes 393224 | tf_op jit(solution)/shard_map/right_swap/ppermute | solution.py:287
  81.0 2.1 %basis.1 = (bf16[128,128]{1,0:T(8,128)(2,1)S(1)}, bf16[512,128]{1,0:T(8,128)(2,1)S(1)}) custom-call(f32[128,128]{1,0:T(8,128)S(1)} %bitcast.17, f32[256,128]{1,0:T(8,128)S(1)} %bitcast.12), custom_call_target="tpu_custom_call" | custom-call | flops 1000 | bytes 1000 | tf_op jit(solution)/shard_map/basis/pallas_call | solution.py:289
  83.1 0.0 collective-permute-done.1.own_ref
  83.2 0.0 collective-permute-done.far_ref
  83.2 1.6 %new_error.1 = (f32[256,896]{1,0:T(8,128)}, f32[28,64]{1,0:T(8,128)}) custom-call(s32[1]{0:T(128)} %bitcast.core_ref, bf16[256,896]{1,0:T(8,128)(2,1)S(1)} %copy-done.1, f32[256,896]{1,0:T(8,128)S(1)} %copy-done, bf16[128,128]{1,0:T(8,128)(2,1)S(1)} %get-tuple-element.21.inverse_ref, bf16[512,128]{1,0:T(8,128)(2,1)S(1)} %get-tuple-element.22.basis_ref, ...), custom_call_target="tpu_custom_call" | custom-call | flops 1000 | bytes 1000 | tf_op jit(solution)/shard_map/new_error/pallas_call | solution.py:297
Async XLA Ops:
  0.6 25.6 %copy-start = (f32[256,896]{1,0:T(8,128)S(1)}, f32[256,896]{1,0:T(8,128)}, u32[]{:S(2)}) copy-start(f32[256,896]{1,0:T(8,128)} %error_ref.3) | copy-start | bytes 2752516
  0.6 25.6 %copy-start.1 = (bf16[256,896]{1,0:T(8,128)(2,1)S(1)}, bf16[256,896]{1,0:T(8,128)(2,1)}, u32[]{:S(2)}) copy-start(bf16[256,896]{1,0:T(8,128)(2,1)} %grad_ref.3) | copy-start | bytes 1376260
  22.4 12.7 %all-to-all-start.1 = ((f32[32,4,128]{2,1,0:T(4,128)}), f32[32,4,128]{2,1,0:T(4,128)S(1)}, u32[]{:S(2)}, u32[]{:S(2)}) async-start(f32[32,4,128]{2,1,0:T(4,128)} %bitcast.5), calls=%async_computation.1 | async-start | bytes 131072 | tf_op jit(solution)/shard_map/left_gather/all_to_all | solution.py:264
  64.1 12.4 %all-to-all-start.3 = ((f32[16,16,128]{2,1,0:T(8,128)}), f32[16,16,128]{2,1,0:T(8,128)S(1)}, u32[]{:S(2)}, u32[]{:S(2)}) async-start(f32[16,16,128]{2,1,0:T(8,128)} %bitcast.9), calls=%async_computation.3 | async-start | bytes 262144 | tf_op jit(solution)/shard_map/right_gather/all_to_all | solution.py:285
  67.6 15.5 %collective-permute-start.1 = (f32[256,128]{1,0:T(8,128)S(1)}, f32[256,128]{1,0:T(8,128)S(1)}, u32[]{:S(2)}, u32[]{:S(2)}) collective-permute-start(f32[256,128]{1,0:T(8,128)S(1)} %get-tuple-element.23), channel_id=1, source_target_pairs={{0,0},{16,32},{32,64},{48,96},{64,128},{80,160},{96,192},{112,224}... | collective-permute-start | bytes 393224 | tf_op jit(solution)/shard_map/right_owner/ppermute | solution.py:281
  76.5 6.7 %collective-permute-start = (f32[256,128]{1,0:T(8,128)S(1)}, f32[256,128]{1,0:T(8,128)S(1)}, u32[]{:S(2)}, u32[]{:S(2)}) collective-permute-start(f32[256,128]{1,0:T(8,128)S(1)} %bitcast.11), channel_id=1, source_target_pairs={{0,1},{1,0},{2,3},{3,2},{4,5},{5,4},{6,7},{7,6},{8,9},{9,8},{10,11... | collective-permute-start | bytes 393224 | tf_op jit(solution)/shard_map/right_swap/ppermute | solution.py:287

commit v4 on v3

--- a/solution.py
+++ b/solution.py
@@ -67,57 +67,84 @@
     out_ref[...] = jnp.concatenate([p[:half], p[half:]], axis=1)
 
 
-def arrange_kernel(grad_ref, error_ref, first_high_ref, first_low_ref, last_high_ref, last_low_ref):
+def arrange_kernel(core_ref, grad_ref, error_ref, first_high_ref, first_low_ref, last_high_ref, last_low_ref, other_ref):
     high, low = split(grad_ref[...].astype(F32) + error_ref[...])
-    shape = (PARTS * SLOT, high.shape[1])
+    core = core_ref[0]
+    shape = (HALF * SLOT, high.shape[1])
     row = lax.broadcasted_iota(jnp.int32, shape, 0)
     col = lax.broadcasted_iota(jnp.int32, shape, 1)
     within = row % SLOT
-    place = OWN * (row // SLOT) + within
-    first = (col == place).astype(F32).astype(BF16)
-    last = ((col == place + SLOT) & (within < OWN - SLOT)).astype(F32).astype(BF16)
-    first_high_ref[...] = dot(first, high, NT).astype(BF16)
-    first_low_ref[...] = dot(first, low, NT).astype(BF16)
-    last_high_ref[...] = dot(last, high, NT).astype(BF16)
-    last_low_ref[...] = dot(last, low, NT).astype(BF16)
+    offset = col - OWN * CORES * (row // SLOT) - within
+
+    def pick(core):
+        place = offset - OWN * core
+        first = (place == 0).astype(F32).astype(BF16)
+        last = ((place == SLOT) & (within < OWN - SLOT)).astype(F32).astype(BF16)
+        return [dot(rows, part, NT) for rows in (first, last) for part in (high, low)]
+
+    for ref, value in zip((first_high_ref, first_low_ref, last_high_ref, last_low_ref), pick(core)):
+        ref[...] = value.astype(BF16)
+    first_high, first_low, last_high, last_low = pick(1 - core)
+    other_ref[: HALF * SLOT] = first_high + first_low
+    other_ref[HALF * SLOT :] = last_high + last_low
 
 
 def sum_left_kernel(in_ref, out_ref):
     rows = in_ref.shape[0]
     total = jnp.sum(in_ref[...].reshape(rows // 8, 8, 128), axis=0)
     total = total + pltpu.roll(total, 4, 0)
-    out_ref[...] = jnp.broadcast_to(total[None], (rows // 8, 8, 128)).reshape(rows, 128)
-
-
-def right_kernel(p_ref, first_high_ref, first_low_ref, last_high_ref, last_low_ref, out_ref, gram_ref):
-    top = p_ref[...]
+    for i in range(out_ref.shape[0] // 8):
+        out_ref[8 * i : 8 * i + 8] = total
+
+
+def spread_left(top):
     bottom = pltpu.roll(top, RANK, 1)
-    lane = lax.broadcasted_iota(jnp.int32, top.shape, 1)
-    lower = lane < RANK
+    lower = lax.broadcasted_iota(jnp.int32, top.shape, 1) < RANK
     zero = jnp.zeros_like(top)
     left = jnp.concatenate([jnp.where(lower, top, zero), jnp.where(lower, bottom, zero)], axis=0)
     right = jnp.concatenate([jnp.where(lower, zero, bottom), jnp.where(lower, zero, top)], axis=0)
-    left_high, left_low = split(left)
-    right_high, right_low = split(right)
-    left_both = jnp.concatenate([left_high, left_low], axis=1)
-    right_both = jnp.concatenate([right_high, right_low], axis=1)
-    both = (
-        dot(first_high_ref[...], left_both, NN)
-        + dot(last_high_ref[...], right_both, NN)
-        + dot(first_low_ref[...], left_both, NN)
-        + dot(last_low_ref[...], right_both, NN)
+    return left, right
+
+
+def right_kernel(core_ref, parts_ref, first_high_ref, first_low_ref, last_high_ref, last_low_ref, other_ref, out_ref, p_ref, gram_ref):
+    half = parts_ref.shape[0] // 2
+    swapped = core_ref[0] == 1
+    zero_p = parts_ref[:half]
+    one_p = parts_ref[half:]
+    near = jnp.where(swapped, one_p, zero_p)
+    p_ref[...] = near
+    first_high, first_low = split(other_ref[: HALF * SLOT])
+    last_high, last_low = split(other_ref[HALF * SLOT :])
+    blocks = (
+        (near, first_high_ref[...], first_low_ref[...], last_high_ref[...], last_low_ref[...]),
+        (jnp.where(swapped, zero_p, one_p), first_high, first_low, last_high, last_low),
     )
+    both = None
+    for p, first_high, first_low, last_high, last_low in blocks:
+        left, right = spread_left(p)
+        left_both = jnp.concatenate(split(left), axis=1)
+        right_both = jnp.concatenate(split(right), axis=1)
+        term = (
+            dot(first_high, left_both, NN)
+            + dot(last_high, right_both, NN)
+            + dot(first_low, left_both, NN)
+            + dot(last_low, right_both, NN)
+        )
+        both = term if both is None else both + term
     out_ref[...] = both[:, :128] + both[:, 128:]
-    turned = top.T
-    turned = jnp.concatenate([turned[:RANK], turned[RANK:]], axis=1)
-    gram_ref[...] = dot3(turned, right, NN)
-    for k in range(PARTS):
-        first = 4 * (k // CORES)
-        out_ref[SLOT * k + 12 : SLOT * k + 16, RANK:] = gram_ref[first : first + 4, RANK:]
+    gram = None
+    for p in (zero_p, one_p):
+        turned = p.T
+        turned = jnp.concatenate([turned[:RANK], turned[RANK:]], axis=1)
+        term = dot3(turned, spread_left(p)[1], NN)
+        gram = term if gram is None else gram + term
+    gram_ref[...] = gram
+    for h in range(HALF):
+        out_ref[SLOT * h + 12 : SLOT * h + 16, RANK:] = gram_ref[4 * h : 4 * h + 4, RANK:]
 
 
 def sum_right_kernel(in_ref, out_ref, own_ref):
-    total = jnp.sum(in_ref[...].reshape(PARTS, SLOT, 128), axis=0)
+    total = jnp.sum(in_ref[...].reshape(HALF, SLOT, 128), axis=0)
     own_ref[...] = jnp.broadcast_to(total[None], (PAYLOAD // SLOT, SLOT, 128)).reshape(PAYLOAD, 128)
     out_ref[...] = jnp.broadcast_to(total[None], (HALF, SLOT, 128)).reshape(HALF * SLOT, 128)
 
@@ -250,27 +277,32 @@
         )(col, grad, error, q_start.T)
     with jax.named_scope("arrange"):
         p_own, grad, error = lax.optimization_barrier((p_own, grad, error))
-        arranged = pl.pallas_call(
+        *arranged, other = pl.pallas_call(
             arrange_kernel,
-            out_shape=[shape(PARTS * SLOT, rows, kind=BF16)] * 4,
+            in_specs=[smem, vmem, vmem],
+            out_shape=[shape(HALF * SLOT, rows, kind=BF16)] * 4 + [shape(2 * HALF * SLOT, rows)],
             compiler_params=params(),
             cost_estimate=cost(2 * 4 * 512 * 256 * 896, 2500000),
-        )(grad, error)
+        )(core, grad, error)
     with jax.named_scope("left_scatter"):
         p_parts = lax.all_to_all(p_own, ("rep", "col"), 0, 0, tiled=True)
     with jax.named_scope("left_sum"):
-        p_sum = pl.pallas_call(sum_left_kernel, out_shape=shape(rows // 2, 128), compiler_params=params())(p_parts)
+        p_sum = pl.pallas_call(sum_left_kernel, out_shape=shape(rows, 128), compiler_params=params())(p_parts)
+    p_sum, other = lax.optimization_barrier((p_sum, other))
     with jax.named_scope("left_gather"):
-        p = lax.all_to_all(p_sum, ("rep", "col"), 0, 0, tiled=True)
+        p_both = lax.all_to_all(p_sum, ("core", "rep", "col"), 0, 0, tiled=True)
+    with jax.named_scope("exchange"):
+        other = lax.ppermute(other, "core", [(0, 1), (1, 0)])
     with jax.named_scope("right"):
-        s_own = pl.pallas_call(
+        s_own, p = pl.pallas_call(
             right_kernel,
-            out_shape=shape(PARTS * SLOT, 128),
+            in_specs=[smem] + [vmem] * 6,
+            out_shape=[shape(HALF * SLOT, 128), shape(rows // 2, 128)],
             scratch_shapes=[pltpu.VMEM((RANK, 128), F32)],
             compiler_params=params(),
-        )(p, *arranged)
+        )(core, p_both, *arranged, other)
     with jax.named_scope("right_scatter"):
-        s_parts = lax.all_to_all(s_own, ("rep", "z", "core"), 0, 0, tiled=True)
+        s_parts = lax.all_to_all(s_own, ("rep", "z"), 0, 0, tiled=True)
     with jax.named_scope("right_sum"):
         s_sum, s_piece = pl.pallas_call(
             sum_right_kernel,

time: 85.2 us -> 83.6 us (0.981)
  blocking collectives: 46.9 us -> 33.7 us
  starting transfers between devices: 12.6 us -> 23.9 us
    all_to_all x2, blocking collectives: 46.9 us -> 33.7 us  [the longest x1 19.5 us: shards(): s_parts = lax.all_to_all(s_own, ('rep', 'z'), 0, 0, tiled=True)]
    all_to_all x1, starting transfers between devices: 3.85 us -> 10.5 us  [shards(): p_parts = lax.all_to_all(p_own, ('rep', 'col'), 0, 0, tiled=True)]
    ppermute x0 -> x1, starting transfers between devices: none -> 4.01 us  [shards(): other = lax.ppermute(other, 'core', [(0, 1), (1, 0)])]
  transfers between devices with their start and end apart: 4 -> 5, of which waited for: 2 -> 2; matrix products, arithmetic and copies ran while one was open for 0% -> 0% of each run, Pallas kernels for 4% -> 4%
where the time goes in v4:
time: 83.6 us; the launch traced here: 83.1 us
  blocking collectives  33.7 us (40%)
  starting transfers between devices  23.9 us (29%)
  waiting for transfers between devices  15.8 us (19%)
  Pallas kernels  8.96 us (11%)
    all_to_all x1, blocking collectives, shards(): s_parts = lax.all_to_all(s_own, ('rep', 'z'), 0, 0, tiled=True)  19.5 us
    all_to_all x1, blocking collectives, shards(): p_both = lax.all_to_all(p_sum, ('core', 'rep', 'col'), 0, 0, tiled=True)  14.3 us
    all_to_all x1, starting transfers between devices, shards(): p_parts = lax.all_to_all(p_own, ('rep', 'col'), 0, 0, tiled=True)  10.5 us
    all_to_all x1, waiting for transfers between devices, shards(): near = lax.all_to_all(s_sum, ('rep', 'z'), 0, 0, tiled=True)  8.3 us
    all_to_all x1, waiting for transfers between devices, shards(): p_parts = lax.all_to_all(p_own, ('rep', 'col'), 0, 0, tiled=True)  7.48 us
    ppermute x1, starting transfers between devices, shards(): far = lax.ppermute(near, 'core', [(0, 1), (1, 0)])  5.2 us
    ppermute x1, starting transfers between devices, shards(): other = lax.ppermute(other, 'core', [(0, 1), (1, 0)])  4.01 us
    all_to_all x1, starting transfers between devices, shards(): near = lax.all_to_all(s_sum, ('rep', 'z'), 0, 0, tiled=True)  3.51 us
  transfers between devices with their start and end apart: 5, of which 2 were waited for; matrix products, arithmetic and copies ran while one was open for 0% of the time, Pallas kernels for 4%

profile of v4, /device:TPU:1, one launch (start us, length us, event | category | flops | bytes accessed | tf_op | source)
XLA Modules:
  0.0 83.1 jit_solution(18037261988924301921)
XLA Ops:
  0.6 0.0 copy-start
  0.6 0.0 copy-start.1
  0.7 2.5 %left.1 = f32[128,128]{1,0:T(8,128)} custom-call(s32[1]{0:T(128)} %bitcast.1.col_ref, bf16[256,896]{1,0:T(8,128)(2,1)} %grad_ref.3, f32[256,896]{1,0:T(8,128)} %error_ref.3, bf16[64,14336]{1,0:T(8,128)(2,1)} %bitcast.19), custom_call_target="tpu_custom_call" | custom-call | tf_op jit(solution)/shard_map/left/pallas_call | solution.py:265
  3.2 10.5 %all-to-all-start = ((f32[32,4,128]{2,1,0:T(4,128)}), f32[32,4,128]{2,1,0:T(4,128)S(1)}, u32[]{:S(2)}, u32[]{:S(2)}) async-start(f32[32,4,128]{2,1,0:T(4,128)} %bitcast.3), calls=%async_computation | async-start | bytes 131072 | tf_op jit(solution)/shard_map/left_scatter/all_to_all | solution.py:288
  13.7 0.0 copy-done
  13.7 0.0 copy-done.1
  13.8 1.3 %arrange.1 = (bf16[256,256]{1,0:T(8,128)(2,1)S(1)}, bf16[256,256]{1,0:T(8,128)(2,1)S(1)}, bf16[256,256]{1,0:T(8,128)(2,1)S(1)}, bf16[256,256]{1,0:T(8,128)(2,1)S(1)}, f32[512,256]{1,0:T(8,128)S(1)}) custom-call(s32[1]{0:T(128)} %bitcast.core_ref, bf16[256,896]{1,0:T(8,128)(2,1)S(1)} %copy-done.1, f32[256,896]{1,0:T(8,128)S(1)} %copy-done), custom_call_target="tpu_custom_call" | custom-call | flops 939524096 | bytes 2500000 | tf_op jit(solution)/shard_map/arrange/pallas_call | solution.py:280
  15.1 7.5 %all-to-all-done = f32[32,4,128]{2,1,0:T(4,128)S(1)} async-done(((f32[32,4,128]{2,1,0:T(4,128)}), f32[32,4,128]{2,1,0:T(4,128)S(1)}, u32[]{:S(2)}, u32[]{:S(2)}) %all-to-all-start) | async-done | bytes 65568 | tf_op jit(solution)/shard_map/left_scatter/all_to_all | solution.py:288
  22.6 4.0 %collective-permute-start = (f32[512,256]{1,0:T(8,128)S(1)}, f32[512,256]{1,0:T(8,128)S(1)}, u32[]{:S(2)}, u32[]{:S(2)}) collective-permute-start(f32[512,256]{1,0:T(8,128)S(1)} %get-tuple-element.27), channel_id=1, source_target_pairs={{0,1},{1,0},{2,3},{3,2},{4,5},{5,4},{6,7},{7,6},{8,9},{9,8},{10,11... | collective-permute-start | bytes 1572872 | tf_op jit(solution)/shard_map/exchange/ppermute | solution.py:295
  26.6 14.3 %all_to_all.44 = f32[64,4,128]{2,1,0:T(4,128)S(1)} all-to-all(f32[64,4,128]{2,1,0:T(4,128)S(1)} %bitcast.15), channel_id=1, replica_groups=mesh['rep'=2,'col'=16,'z'=8,'core'=2] {'core','rep','col'}, dimensions={0} | all-to-all | bytes 262144 | tf_op jit(solution)/shard_map/left_gather/all_to_all | solution.py:293
  40.9 0.0 collective-permute-done.other_ref
  40.9 0.6 right.1
  41.5 19.5 %all_to_all.45 = f32[16,16,128]{2,1,0:T(8,128)S(1)} all-to-all(f32[16,16,128]{2,1,0:T(8,128)S(1)} %bitcast.18), channel_id=1, replica_groups=mesh['rep'=2,'col'=16,'z'=8,'core'=2] {'rep','z'}, dimensions={0} | all-to-all | bytes 262144 | tf_op jit(solution)/shard_map/right_scatter/all_to_all | solution.py:305
  61.0 0.7 right_sum.1
  61.7 3.5 %all-to-all-start.3 = ((f32[16,16,128]{2,1,0:T(8,128)}), f32[16,16,128]{2,1,0:T(8,128)S(1)}, u32[]{:S(2)}, u32[]{:S(2)}) async-start(f32[16,16,128]{2,1,0:T(8,128)} %bitcast.9), calls=%async_computation.3 | async-start | bytes 262144 | tf_op jit(solution)/shard_map/right_gather/all_to_all | solution.py:317
  65.2 0.7 collective-permute-start.2
  65.9 8.3 %all-to-all-done.3 = f32[16,16,128]{2,1,0:T(8,128)S(1)} async-done(((f32[16,16,128]{2,1,0:T(8,128)}), f32[16,16,128]{2,1,0:T(8,128)S(1)}, u32[]{:S(2)}, u32[]{:S(2)}) %all-to-all-start.3) | async-done | bytes 131104 | tf_op jit(solution)/shard_map/right_gather/all_to_all | solution.py:317
  74.2 5.2 %collective-permute-start.1 = (f32[256,128]{1,0:T(8,128)S(1)}, f32[256,128]{1,0:T(8,128)S(1)}, u32[]{:S(2)}, u32[]{:S(2)}) collective-permute-start(f32[256,128]{1,0:T(8,128)S(1)} %bitcast.11), channel_id=1, source_target_pairs={{0,1},{1,0},{2,3},{3,2},{4,5},{5,4},{6,7},{7,6},{8,9},{9,8},{10,11... | collective-permute-start | bytes 393224 | tf_op jit(solution)/shard_map/right_swap/ppermute | solution.py:319
  79.4 2.1 %basis.1 = (bf16[128,128]{1,0:T(8,128)(2,1)S(1)}, bf16[512,128]{1,0:T(8,128)(2,1)S(1)}) custom-call(f32[128,128]{1,0:T(8,128)S(1)} %get-tuple-element.28.p_ref, f32[256,128]{1,0:T(8,128)S(1)} %bitcast.12), custom_call_target="tpu_custom_call" | custom-call | flops 1000 | bytes 1000 | tf_op jit(solution)/shard_map/basis/pallas_call | solution.py:321
  81.5 0.0 collective-permute-done.2.own_ref
  81.5 0.0 collective-permute-done.1.far_ref
  81.5 1.6 %new_error.1 = (f32[256,896]{1,0:T(8,128)}, f32[28,64]{1,0:T(8,128)}) custom-call(s32[1]{0:T(128)} %bitcast.core_ref, bf16[256,896]{1,0:T(8,128)(2,1)S(1)} %copy-done.1, f32[256,896]{1,0:T(8,128)S(1)} %copy-done, bf16[128,128]{1,0:T(8,128)(2,1)S(1)} %get-tuple-element.31.inverse_ref, bf16[512,128]{1,0:T(8,128)(2,1)S(1)} %get-tuple-element.32.basis_ref, ...), custom_call_target="tpu_custom_call" | custom-call | flops 1000 | bytes 1000 | tf_op jit(solution)/shard_map/new_error/pallas_call | solution.py:329
  (1 shorter events, 0.0 us)
Async XLA Ops:
  0.6 13.1 %copy-start = (f32[256,896]{1,0:T(8,128)S(1)}, f32[256,896]{1,0:T(8,128)}, u32[]{:S(2)}) copy-start(f32[256,896]{1,0:T(8,128)} %error_ref.3) | copy-start | bytes 2752516
  0.6 13.1 %copy-start.1 = (bf16[256,896]{1,0:T(8,128)(2,1)S(1)}, bf16[256,896]{1,0:T(8,128)(2,1)}, u32[]{:S(2)}) copy-start(bf16[256,896]{1,0:T(8,128)(2,1)} %grad_ref.3) | copy-start | bytes 1376260
  3.2 19.4 %all-to-all-start = ((f32[32,4,128]{2,1,0:T(4,128)}), f32[32,4,128]{2,1,0:T(4,128)S(1)}, u32[]{:S(2)}, u32[]{:S(2)}) async-start(f32[32,4,128]{2,1,0:T(4,128)} %bitcast.3), calls=%async_computation | async-start | bytes 131072 | tf_op jit(solution)/shard_map/left_scatter/all_to_all | solution.py:288
  22.6 18.3 %collective-permute-start = (f32[512,256]{1,0:T(8,128)S(1)}, f32[512,256]{1,0:T(8,128)S(1)}, u32[]{:S(2)}, u32[]{:S(2)}) collective-permute-start(f32[512,256]{1,0:T(8,128)S(1)} %get-tuple-element.27), channel_id=1, source_target_pairs={{0,1},{1,0},{2,3},{3,2},{4,5},{5,4},{6,7},{7,6},{8,9},{9,8},{10,11... | collective-permute-start | bytes 1572872 | tf_op jit(solution)/shard_map/exchange/ppermute | solution.py:295
  61.7 12.5 %all-to-all-start.3 = ((f32[16,16,128]{2,1,0:T(8,128)}), f32[16,16,128]{2,1,0:T(8,128)S(1)}, u32[]{:S(2)}, u32[]{:S(2)}) async-start(f32[16,16,128]{2,1,0:T(8,128)} %bitcast.9), calls=%async_computation.3 | async-start | bytes 262144 | tf_op jit(solution)/shard_map/right_gather/all_to_all | solution.py:317
  65.2 16.3 %collective-permute-start.2 = (f32[256,128]{1,0:T(8,128)S(1)}, f32[256,128]{1,0:T(8,128)S(1)}, u32[]{:S(2)}, u32[]{:S(2)}) collective-permute-start(f32[256,128]{1,0:T(8,128)S(1)} %get-tuple-element.33), channel_id=1, source_target_pairs={{0,0},{16,32},{32,64},{48,96},{64,128},{80,160},{96,192},{112,224}... | collective-permute-start | bytes 393224 | tf_op jit(solution)/shard_map/right_owner/ppermute | solution.py:313
  74.2 7.3 %collective-permute-start.1 = (f32[256,128]{1,0:T(8,128)S(1)}, f32[256,128]{1,0:T(8,128)S(1)}, u32[]{:S(2)}, u32[]{:S(2)}) collective-permute-start(f32[256,128]{1,0:T(8,128)S(1)} %bitcast.11), channel_id=1, source_target_pairs={{0,1},{1,0},{2,3},{3,2},{4,5},{5,4},{6,7},{7,6},{8,9},{9,8},{10,11... | collective-permute-start | bytes 393224 | tf_op jit(solution)/shard_map/right_swap/ppermute | solution.py:319

commit v5 on v4

--- a/solution.py
+++ b/solution.py
@@ -12,10 +12,12 @@
 CORES = 2
 HALF = PARTS // CORES
 CHUNKS = 2
+SENDS = (320, 128)
 LEFT_LIMIT = 54912
 PAYLOAD = 256
 WIDTH = 8
 SLOT = 16
+TAIL = 12
 NT = (((1,), (1,)), ((), ()))
 NN = (((1,), (0,)), ((), ()))
 BF16 = jnp.bfloat16
@@ -67,7 +69,7 @@
     out_ref[...] = jnp.concatenate([p[:half], p[half:]], axis=1)
 
 
-def arrange_kernel(core_ref, grad_ref, error_ref, first_high_ref, first_low_ref, last_high_ref, last_low_ref, other_ref):
+def arrange_kernel(core_ref, grad_ref, error_ref, first_high_ref, first_low_ref, last_high_ref, last_low_ref, *other_refs):
     high, low = split(grad_ref[...].astype(F32) + error_ref[...])
     core = core_ref[0]
     shape = (HALF * SLOT, high.shape[1])
@@ -84,9 +86,17 @@
 
     for ref, value in zip((first_high_ref, first_low_ref, last_high_ref, last_low_ref), pick(core)):
         ref[...] = value.astype(BF16)
-    first_high, first_low, last_high, last_low = pick(1 - core)
-    other_ref[: HALF * SLOT] = first_high + first_low
-    other_ref[HALF * SLOT :] = last_high + last_low
+    shape = (HALF * TAIL, high.shape[1])
+    row = lax.broadcasted_iota(jnp.int32, shape, 0)
+    col = lax.broadcasted_iota(jnp.int32, shape, 1)
+    place = OWN * (CORES * (row // TAIL) + 1 - core) + SLOT + row % TAIL
+    tail = (col == place).astype(F32).astype(BF16)
+    first_high, first_low = pick(1 - core)[:2]
+    other = jnp.concatenate([first_high + first_low, dot(tail, high, NT) + dot(tail, low, NT)], axis=0)
+    start = 0
+    for size, ref in zip(SENDS, other_refs):
+        ref[...] = other[start : start + size]
+        start += size
 
 
 def sum_left_kernel(in_ref, out_ref):
@@ -106,32 +116,36 @@
     return left, right
 
 
-def right_kernel(core_ref, parts_ref, first_high_ref, first_low_ref, last_high_ref, last_low_ref, other_ref, out_ref, p_ref, gram_ref):
+def right_kernel(core_ref, parts_ref, first_high_ref, first_low_ref, last_high_ref, last_low_ref, *refs):
+    *other_refs, out_ref, p_ref, gram_ref = refs
     half = parts_ref.shape[0] // 2
     swapped = core_ref[0] == 1
     zero_p = parts_ref[:half]
     one_p = parts_ref[half:]
     near = jnp.where(swapped, one_p, zero_p)
     p_ref[...] = near
-    first_high, first_low = split(other_ref[: HALF * SLOT])
-    last_high, last_low = split(other_ref[HALF * SLOT :])
-    blocks = (
-        (near, first_high_ref[...], first_low_ref[...], last_high_ref[...], last_low_ref[...]),
-        (jnp.where(swapped, zero_p, one_p), first_high, first_low, last_high, last_low),
+    other = jnp.concatenate([ref[...] for ref in other_refs], axis=0)
+    first_high, first_low = split(other[: HALF * SLOT])
+    last_high, last_low = split(other[HALF * SLOT :])
+    left, right = spread_left(near)
+    left = jnp.concatenate(split(left), axis=1)
+    right = jnp.concatenate(split(right), axis=1)
+    both = (
+        dot(first_high_ref[...], left, NN)
+        + dot(last_high_ref[...], right, NN)
+        + dot(first_low_ref[...], left, NN)
+        + dot(last_low_ref[...], right, NN)
     )
-    both = None
-    for p, first_high, first_low, last_high, last_low in blocks:
-        left, right = spread_left(p)
-        left_both = jnp.concatenate(split(left), axis=1)
-        right_both = jnp.concatenate(split(right), axis=1)
-        term = (
-            dot(first_high, left_both, NN)
-            + dot(last_high, right_both, NN)
-            + dot(first_low, left_both, NN)
-            + dot(last_low, right_both, NN)
-        )
-        both = term if both is None else both + term
+    left, right = spread_left(jnp.where(swapped, zero_p, one_p))
+    left = jnp.concatenate(split(left), axis=1)
+    right = jnp.concatenate(split(right), axis=1)
+    both = both + dot(first_high, left, NN) + dot(first_low, left, NN)
+    tail = dot(last_high, right, NN) + dot(last_low, right, NN)
     out_ref[...] = both[:, :128] + both[:, 128:]
+    tail = tail[:, :128] + tail[:, 128:]
+    for h in range(HALF):
+        part = slice(SLOT * h, SLOT * h + TAIL)
+        out_ref[part, :] = out_ref[part, :] + tail[TAIL * h : TAIL * h + TAIL]
     gram = None
     for p in (zero_p, one_p):
         turned = p.T
@@ -277,10 +291,10 @@
         )(col, grad, error, q_start.T)
     with jax.named_scope("arrange"):
         p_own, grad, error = lax.optimization_barrier((p_own, grad, error))
-        *arranged, other = pl.pallas_call(
+        arranged = pl.pallas_call(
             arrange_kernel,
             in_specs=[smem, vmem, vmem],
-            out_shape=[shape(HALF * SLOT, rows, kind=BF16)] * 4 + [shape(2 * HALF * SLOT, rows)],
+            out_shape=[shape(HALF * SLOT, rows, kind=BF16)] * 4 + [shape(size, rows) for size in SENDS],
             compiler_params=params(),
             cost_estimate=cost(2 * 4 * 512 * 256 * 896, 2500000),
         )(core, grad, error)
@@ -288,19 +302,19 @@
         p_parts = lax.all_to_all(p_own, ("rep", "col"), 0, 0, tiled=True)
     with jax.named_scope("left_sum"):
         p_sum = pl.pallas_call(sum_left_kernel, out_shape=shape(rows, 128), compiler_params=params())(p_parts)
-    p_sum, other = lax.optimization_barrier((p_sum, other))
+    p_sum, late = lax.optimization_barrier((p_sum, arranged[5:]))
     with jax.named_scope("left_gather"):
         p_both = lax.all_to_all(p_sum, ("core", "rep", "col"), 0, 0, tiled=True)
     with jax.named_scope("exchange"):
-        other = lax.ppermute(other, "core", [(0, 1), (1, 0)])
+        other = [lax.ppermute(part, "core", [(0, 1), (1, 0)]) for part in [*arranged[4:5], *late]]
     with jax.named_scope("right"):
         s_own, p = pl.pallas_call(
             right_kernel,
-            in_specs=[smem] + [vmem] * 6,
+            in_specs=[smem] + [vmem] * (5 + len(SENDS)),
             out_shape=[shape(HALF * SLOT, 128), shape(rows // 2, 128)],
             scratch_shapes=[pltpu.VMEM((RANK, 128), F32)],
             compiler_params=params(),
-        )(core, p_both, *arranged, other)
+        )(core, p_both, *arranged[:4], *other)
     with jax.named_scope("right_scatter"):
         s_parts = lax.all_to_all(s_own, ("rep", "z"), 0, 0, tiled=True)
     with jax.named_scope("right_sum"):

time: 83.6 us -> 83 us (level)
  blocking collectives: 33.7 us -> 19.5 us
  starting transfers between devices: 23.9 us -> 31.4 us
  waiting for transfers between devices: 15.8 us -> 21.3 us
    all_to_all x1 -> x0, blocking collectives: 14.3 us -> none  [shards(): p_both = lax.all_to_all(p_sum, ('core', 'rep', 'col'), 0, 0, tiled=True)]
    all_to_all x0 -> x1, waiting for transfers between devices: none -> 7.49 us  [shards(): p_both = lax.all_to_all(p_sum, ('core', 'rep', 'col'), 0, 0, tiled=True)]
    all_to_all x0 -> x1, starting transfers between devices: none -> 6.37 us  [shards(): p_both = lax.all_to_all(p_sum, ('core', 'rep', 'col'), 0, 0, tiled=True)]
    all_to_all x1, waiting for transfers between devices: 7.48 us -> 4.57 us  [shards(): p_parts = lax.all_to_all(p_own, ('rep', 'col'), 0, 0, tiled=True)]
    ppermute x1 -> x2, starting transfers between devices: 4.01 us -> 5.12 us  [shards(): lax.ppermute(part, 'core', [(0, 1), (1, 0)])]
    ppermute x1 -> x2, waiting for transfers between devices: 0.01 us -> 0.97 us  [shards(): lax.ppermute(part, 'core', [(0, 1), (1, 0)])]
  transfers between devices with their start and end apart: 5 -> 7, of which waited for: 2 -> 4; matrix products, arithmetic and copies ran while one was open for 0% -> 0% of each run, Pallas kernels for 4% -> 5%
where the time goes in v5:
time: 83 us; the launch traced here: 82.6 us
  starting transfers between devices  31.4 us (38%)
  waiting for transfers between devices  21.3 us (26%)
  blocking collectives  19.5 us (23%)
  Pallas kernels  9.61 us (12%)
    all_to_all x1, blocking collectives, shards(): s_parts = lax.all_to_all(s_own, ('rep', 'z'), 0, 0, tiled=True)  19.5 us
    all_to_all x1, starting transfers between devices, shards(): p_parts = lax.all_to_all(p_own, ('rep', 'col'), 0, 0, tiled=True)  10.5 us
    all_to_all x1, waiting for transfers between devices, shards(): near = lax.all_to_all(s_sum, ('rep', 'z'), 0, 0, tiled=True)  8.29 us
    all_to_all x1, waiting for transfers between devices, shards(): p_both = lax.all_to_all(p_sum, ('core', 'rep', 'col'), 0, 0, tiled=True)  7.49 us
    all_to_all x1, starting transfers between devices, shards(): p_both = lax.all_to_all(p_sum, ('core', 'rep', 'col'), 0, 0, tiled=True)  6.37 us
    ppermute x1, starting transfers between devices, shards(): far = lax.ppermute(near, 'core', [(0, 1), (1, 0)])  5.21 us
    ppermute x2, starting transfers between devices, shards(): lax.ppermute(part, 'core', [(0, 1), (1, 0)])  5.12 us
    all_to_all x1, waiting for transfers between devices, shards(): p_parts = lax.all_to_all(p_own, ('rep', 'col'), 0, 0, tiled=True)  4.57 us
  transfers between devices with their start and end apart: 7, of which 4 were waited for; matrix products, arithmetic and copies ran while one was open for 0% of the time, Pallas kernels for 5%

profile of v5, /device:TPU:1, one launch (start us, length us, event | category | flops | bytes accessed | tf_op | source)
XLA Modules:
  0.0 82.6 jit_solution(7313333720748496556)
XLA Ops:
  0.6 0.0 copy-start
  0.6 0.0 copy-start.1
  0.7 2.5 %left.1 = f32[128,128]{1,0:T(8,128)} custom-call(s32[1]{0:T(128)} %bitcast.1.col_ref, bf16[256,896]{1,0:T(8,128)(2,1)} %grad_ref.3, f32[256,896]{1,0:T(8,128)} %error_ref.3, bf16[64,14336]{1,0:T(8,128)(2,1)} %bitcast.18), custom_call_target="tpu_custom_call" | custom-call | tf_op jit(solution)/shard_map/left/pallas_call | solution.py:279
  3.2 10.5 %all-to-all-start = ((f32[32,4,128]{2,1,0:T(4,128)}), f32[32,4,128]{2,1,0:T(4,128)S(1)}, u32[]{:S(2)}, u32[]{:S(2)}) async-start(f32[32,4,128]{2,1,0:T(4,128)} %bitcast.3), calls=%async_computation | async-start | bytes 131072 | tf_op jit(solution)/shard_map/left_scatter/all_to_all | solution.py:302
  13.7 0.0 copy-done
  13.7 0.0 copy-done.1
  13.8 1.4 %arrange.1 = (bf16[256,256]{1,0:T(8,128)(2,1)S(1)}, bf16[256,256]{1,0:T(8,128)(2,1)S(1)}, bf16[256,256]{1,0:T(8,128)(2,1)S(1)}, bf16[256,256]{1,0:T(8,128)(2,1)S...) custom-call(s32[1]{0:T(128)} %bitcast.core_ref, bf16[256,896]{1,0:T(8,128)(2,1)S(1)} %copy-done.1, f32[256,896]{1,0:T(8,128)S(1)} %copy-done), custom_call_target="tpu_custom_call" | custom-call | flops 939524096 | bytes 2500000 | tf_op jit(solution)/shard_map/arrange/pallas_call | solution.py:294
  15.1 2.9 %collective-permute-start = (f32[320,256]{1,0:T(8,128)S(1)}, f32[320,256]{1,0:T(8,128)S(1)}, u32[]{:S(2)}, u32[]{:S(2)}) collective-permute-start(f32[320,256]{1,0:T(8,128)S(1)} %get-tuple-element.28), channel_id=1, source_target_pairs={{0,1},{1,0},{2,3},{3,2},{4,5},{5,4},{6,7},{7,6},{8,9},{9,8},{10,11... | collective-permute-start | bytes 983048 | tf_op jit(solution)/shard_map/exchange/ppermute | solution.py:309
  18.0 4.6 %all-to-all-done = f32[32,4,128]{2,1,0:T(4,128)S(1)} async-done(((f32[32,4,128]{2,1,0:T(4,128)}), f32[32,4,128]{2,1,0:T(4,128)S(1)}, u32[]{:S(2)}, u32[]{:S(2)}) %all-to-all-start) | async-done | bytes 65568 | tf_op jit(solution)/shard_map/left_scatter/all_to_all | solution.py:302
  22.6 0.7 left_sum.1
  23.3 6.4 %all-to-all-start.1 = ((f32[64,4,128]{2,1,0:T(4,128)}), f32[64,4,128]{2,1,0:T(4,128)S(1)}, u32[]{:S(2)}, u32[]{:S(2)}) async-start(f32[64,4,128]{2,1,0:T(4,128)} %bitcast.5), calls=%async_computation.1 | async-start | bytes 262144 | tf_op jit(solution)/shard_map/left_gather/all_to_all | solution.py:307
  29.6 2.3 %collective-permute-start.1 = (f32[128,256]{1,0:T(8,128)S(1)}, f32[128,256]{1,0:T(8,128)S(1)}, u32[]{:S(2)}, u32[]{:S(2)}) collective-permute-start(f32[128,256]{1,0:T(8,128)S(1)} %get-tuple-element.29), channel_id=1, source_target_pairs={{0,1},{1,0},{2,3},{3,2},{4,5},{5,4},{6,7},{7,6},{8,9},{9,8},{10,11... | collective-permute-start | bytes 393224 | tf_op jit(solution)/shard_map/exchange/ppermute | solution.py:309
  31.9 1.0 %collective-permute-done.1.refs_1_ = f32[128,256]{1,0:T(8,128)S(1)} collective-permute-done((f32[128,256]{1,0:T(8,128)S(1)}, f32[128,256]{1,0:T(8,128)S(1)}, u32[]{:S(2)}, u32[]{:S(2)}) %collective-permute-start.1) | collective-permute-done | bytes 131104 | tf_op jit(solution)/shard_map/exchange/ppermute | solution.py:309
  32.9 0.0 collective-permute-done.refs_0_
  32.9 7.5 %all-to-all-done.1 = f32[64,4,128]{2,1,0:T(4,128)S(1)} async-done(((f32[64,4,128]{2,1,0:T(4,128)}), f32[64,4,128]{2,1,0:T(4,128)S(1)}, u32[]{:S(2)}, u32[]{:S(2)}) %all-to-all-start.1) | async-done | bytes 131104 | tf_op jit(solution)/shard_map/left_gather/all_to_all | solution.py:307
  40.4 0.6 right.1
  41.0 19.5 %all_to_all.44 = f32[16,16,128]{2,1,0:T(8,128)S(1)} all-to-all(f32[16,16,128]{2,1,0:T(8,128)S(1)} %bitcast.17), channel_id=1, replica_groups=mesh['rep'=2,'col'=16,'z'=8,'core'=2] {'rep','z'}, dimensions={0} | all-to-all | bytes 262144 | tf_op jit(solution)/shard_map/right_scatter/all_to_all | solution.py:319
  60.4 0.7 right_sum.1
  61.1 3.5 %all-to-all-start.3 = ((f32[16,16,128]{2,1,0:T(8,128)}), f32[16,16,128]{2,1,0:T(8,128)S(1)}, u32[]{:S(2)}, u32[]{:S(2)}) async-start(f32[16,16,128]{2,1,0:T(8,128)} %bitcast.9), calls=%async_computation.3 | async-start | bytes 262144 | tf_op jit(solution)/shard_map/right_gather/all_to_all | solution.py:331
  64.6 0.7 collective-permute-start.3
  65.3 8.3 %all-to-all-done.3 = f32[16,16,128]{2,1,0:T(8,128)S(1)} async-done(((f32[16,16,128]{2,1,0:T(8,128)}), f32[16,16,128]{2,1,0:T(8,128)S(1)}, u32[]{:S(2)}, u32[]{:S(2)}) %all-to-all-start.3) | async-done | bytes 131104 | tf_op jit(solution)/shard_map/right_gather/all_to_all | solution.py:331
  73.6 5.2 %collective-permute-start.2 = (f32[256,128]{1,0:T(8,128)S(1)}, f32[256,128]{1,0:T(8,128)S(1)}, u32[]{:S(2)}, u32[]{:S(2)}) collective-permute-start(f32[256,128]{1,0:T(8,128)S(1)} %bitcast.11), channel_id=1, source_target_pairs={{0,1},{1,0},{2,3},{3,2},{4,5},{5,4},{6,7},{7,6},{8,9},{9,8},{10,11... | collective-permute-start | bytes 393224 | tf_op jit(solution)/shard_map/right_swap/ppermute | solution.py:333
  78.8 2.1 %basis.1 = (bf16[128,128]{1,0:T(8,128)(2,1)S(1)}, bf16[512,128]{1,0:T(8,128)(2,1)S(1)}) custom-call(f32[128,128]{1,0:T(8,128)S(1)} %get-tuple-element.30.p_ref, f32[256,128]{1,0:T(8,128)S(1)} %bitcast.12), custom_call_target="tpu_custom_call" | custom-call | flops 1000 | bytes 1000 | tf_op jit(solution)/shard_map/basis/pallas_call | solution.py:335
  80.9 0.0 collective-permute-done.3.own_ref
  80.9 0.0 collective-permute-done.2.far_ref
  81.0 1.6 %new_error.1 = (f32[256,896]{1,0:T(8,128)}, f32[28,64]{1,0:T(8,128)}) custom-call(s32[1]{0:T(128)} %bitcast.core_ref, bf16[256,896]{1,0:T(8,128)(2,1)S(1)} %copy-done.1, f32[256,896]{1,0:T(8,128)S(1)} %copy-done, bf16[128,128]{1,0:T(8,128)(2,1)S(1)} %get-tuple-element.33.inverse_ref, bf16[512,128]{1,0:T(8,128)(2,1)S(1)} %get-tuple-element.34.basis_ref, ...), custom_call_target="tpu_custom_call" | custom-call | flops 1000 | bytes 1000 | tf_op jit(solution)/shard_map/new_error/pallas_call | solution.py:343
Async XLA Ops:
  0.6 13.1 %copy-start = (f32[256,896]{1,0:T(8,128)S(1)}, f32[256,896]{1,0:T(8,128)}, u32[]{:S(2)}) copy-start(f32[256,896]{1,0:T(8,128)} %error_ref.3) | copy-start | bytes 2752516
  0.6 13.1 %copy-start.1 = (bf16[256,896]{1,0:T(8,128)(2,1)S(1)}, bf16[256,896]{1,0:T(8,128)(2,1)}, u32[]{:S(2)}) copy-start(bf16[256,896]{1,0:T(8,128)(2,1)} %grad_ref.3) | copy-start | bytes 1376260
  3.2 19.4 %all-to-all-start = ((f32[32,4,128]{2,1,0:T(4,128)}), f32[32,4,128]{2,1,0:T(4,128)S(1)}, u32[]{:S(2)}, u32[]{:S(2)}) async-start(f32[32,4,128]{2,1,0:T(4,128)} %bitcast.3), calls=%async_computation | async-start | bytes 131072 | tf_op jit(solution)/shard_map/left_scatter/all_to_all | solution.py:302
  15.1 17.7 %collective-permute-start = (f32[320,256]{1,0:T(8,128)S(1)}, f32[320,256]{1,0:T(8,128)S(1)}, u32[]{:S(2)}, u32[]{:S(2)}) collective-permute-start(f32[320,256]{1,0:T(8,128)S(1)} %get-tuple-element.28), channel_id=1, source_target_pairs={{0,1},{1,0},{2,3},{3,2},{4,5},{5,4},{6,7},{7,6},{8,9},{9,8},{10,11... | collective-permute-start | bytes 983048 | tf_op jit(solution)/shard_map/exchange/ppermute | solution.py:309
  23.3 17.1 %all-to-all-start.1 = ((f32[64,4,128]{2,1,0:T(4,128)}), f32[64,4,128]{2,1,0:T(4,128)S(1)}, u32[]{:S(2)}, u32[]{:S(2)}) async-start(f32[64,4,128]{2,1,0:T(4,128)} %bitcast.5), calls=%async_computation.1 | async-start | bytes 262144 | tf_op jit(solution)/shard_map/left_gather/all_to_all | solution.py:307
  29.6 3.2 %collective-permute-start.1 = (f32[128,256]{1,0:T(8,128)S(1)}, f32[128,256]{1,0:T(8,128)S(1)}, u32[]{:S(2)}, u32[]{:S(2)}) collective-permute-start(f32[128,256]{1,0:T(8,128)S(1)} %get-tuple-element.29), channel_id=1, source_target_pairs={{0,1},{1,0},{2,3},{3,2},{4,5},{5,4},{6,7},{7,6},{8,9},{9,8},{10,11... | collective-permute-start | bytes 393224 | tf_op jit(solution)/shard_map/exchange/ppermute | solution.py:309
  61.1 12.5 %all-to-all-start.3 = ((f32[16,16,128]{2,1,0:T(8,128)}), f32[16,16,128]{2,1,0:T(8,128)S(1)}, u32[]{:S(2)}, u32[]{:S(2)}) async-start(f32[16,16,128]{2,1,0:T(8,128)} %bitcast.9), calls=%async_computation.3 | async-start | bytes 262144 | tf_op jit(solution)/shard_map/right_gather/all_to_all | solution.py:331
  64.6 16.3 %collective-permute-start.3 = (f32[256,128]{1,0:T(8,128)S(1)}, f32[256,128]{1,0:T(8,128)S(1)}, u32[]{:S(2)}, u32[]{:S(2)}) collective-permute-start(f32[256,128]{1,0:T(8,128)S(1)} %get-tuple-element.35), channel_id=1, source_target_pairs={{0,0},{16,32},{32,64},{48,96},{64,128},{80,160},{96,192},{112,224}... | collective-permute-start | bytes 393224 | tf_op jit(solution)/shard_map/right_owner/ppermute | solution.py:327
  73.6 7.3 %collective-permute-start.2 = (f32[256,128]{1,0:T(8,128)S(1)}, f32[256,128]{1,0:T(8,128)S(1)}, u32[]{:S(2)}, u32[]{:S(2)}) collective-permute-start(f32[256,128]{1,0:T(8,128)S(1)} %bitcast.11), channel_id=1, source_target_pairs={{0,1},{1,0},{2,3},{3,2},{4,5},{5,4},{6,7},{7,6},{8,9},{9,8},{10,11... | collective-permute-start | bytes 393224 | tf_op jit(solution)/shard_map/right_swap/ppermute | solution.py:333
